TPU v7x, 32 devices: a whole 2x2x4 slice. The times are simulated.
32 devices in a mesh: tile: 2 (over y), strip: 4 (over x, core), focus: 4 (over z).
Axes of the slice: x: 2, y: 2, z: 4, core: 2. Of those that a mesh axis runs over, the one named last changes fastest.
Arguments:
- phi: float32 [512, 2048], P(('tile', 'strip')), parts along dimension 0, may hold values from -6 to 6
- target: int32 [512, 2048], P(('tile', 'strip')), parts along dimension 0, may hold values 0 or 1
- defocus_ids: int32 [8], P(('tile', 'focus')), parts along dimension 0, may hold values from 0 to 30
- kernels: float32 [2, 4, 48, 512], replicated, may hold values from -16 to 16
- psi: float32 [48, 512], replicated, may hold values from -3.140625 to 3.140625
- row_freqs: int32 [48], replicated, may hold values from -96 to 95, as said below
- col_freqs: int32 [512], replicated, may hold values from -1024 to 1023, as said below
Outputs:
- phi_next: float32 [512, 2048], P(('tile', 'strip')), parts along dimension 0
There are 2 independent parts, one for each index of `tile`. A program takes and returns all parts, laid end to end along the dimension named above; an argument that names none is the same for every part. Nothing has to cross between parts.
Inputs may be any that keep to these rules, and one draw needn't show every extreme that they name: `row_freqs`: distinct whole frequencies; the lowest and highest of the range are always among them. `col_freqs`: distinct whole frequencies; the lowest and highest of the range are always among them.
All inputs are finite; a program needn't handle non-finite values. No bound on the sum of `target` on one device may be relied on, other than what follows from the above.
Results may differ from a plain program's by a relative error of at most 0.02.
Values may be sent and summed in bfloat16 or wider, within the bound.
A program may use at most 64 MiB of HBM per device.

v0:
```python
import jax
import jax.numpy as jnp
from jax import lax
from jax.sharding import PartitionSpec as P

MARGIN = 64
LEVELS = 31
SWEEPS = 2


slope_resist = 4.0
level_resist = 0.5
step_size = 1.0
flow_rate = 0.2


def padded_2(block, sides, width):
    for axis, dim in sides:
        count = lax.axis_size(axis)
        forward = [(i, i + 1) for i in range(count - 1)]
        backward = [(target, source) for source, target in forward]
        low = lax.ppermute(
            lax.slice_in_dim(block, block.shape[dim] - width, None, axis=dim), axis, forward
        )
        high = lax.ppermute(lax.slice_in_dim(block, 0, width, axis=dim), axis, backward)
        block = jnp.concatenate([low, block, high], axis=dim)
    return block


def tables(freq_list, period, length):
    positions = jnp.arange(length, dtype=jnp.int32)
    phase_int = jnp.mod(freq_list[:, None] * positions[None, :], period)
    angles = phase_int.astype(jnp.float32) * (2.0 * jnp.pi / period)
    return (jnp.cos(angles).astype(jnp.bfloat16), jnp.sin(angles).astype(jnp.bfloat16))


def product(lhs_mat, rhs_mat):
    return jnp.dot(lhs_mat, rhs_mat, preferred_element_type=jnp.float32)


def product_t(lhs_mat, rhs_mat):
    return lax.dot_general(
        lhs_mat, rhs_mat, (((1,), (1,)), ((), ())), preferred_element_type=jnp.float32
    )


def exact_t(lhs_mat, rhs_mat):
    return lax.dot_general(
        lhs_mat.astype(jnp.float32),
        rhs_mat,
        (((0,), (0,)), ((), ())),
        precision=lax.Precision.HIGHEST,
        preferred_element_type=jnp.float32,
    )


def spectral_rows(cos_part, sin_part, y_re, y_im):
    z_re = exact_t(cos_part, y_re) - exact_t(sin_part, y_im)
    z_im = exact_t(cos_part, y_im) + exact_t(sin_part, y_re)
    return jnp.concatenate([z_re, z_im], axis=1).astype(jnp.bfloat16)


def curvature_step(extended):
    padded = jnp.pad(extended, ((0, 0), (1, 1)))
    center = padded[1:-1, 1:-1]
    upper_row = padded[2:, 1:-1]
    lower_row = padded[:-2, 1:-1]
    right_col = padded[1:-1, 2:]
    left_col = padded[1:-1, :-2]
    diagonal = padded[2:, 2:] - padded[2:, :-2] - padded[:-2, 2:] + padded[:-2, :-2]
    grad_x = 0.5 * (upper_row - lower_row)
    grad_y = 0.5 * (right_col - left_col)
    second_x = upper_row - 2.0 * center + lower_row
    second_y = right_col - 2.0 * center + left_col
    cross_term = 0.25 * diagonal
    flow_term = (
        second_x * grad_y * grad_y - 2.0 * grad_x * grad_y * cross_term + second_y * grad_x * grad_x
    ) / (1.0 + grad_x * grad_x + grad_y * grad_y)
    return center + flow_rate * flow_term


def on_device(phi, target, defocus_ids, kernels, psi, row_freqs, col_freqs):
    strip_rows, col_count = phi.shape
    spectrum = psi.shape[1]
    kernel_count = kernels.shape[1]
    window_rows = strip_rows + 2 * MARGIN
    scale_norm = 1.0 / jnp.sqrt(jnp.float32(window_rows * col_count))
    row_cos, row_sin = tables(row_freqs, window_rows, window_rows)
    col_cos, col_sin = tables(col_freqs, col_count, col_count)
    forward = jnp.concatenate([col_cos, -col_sin], axis=0)
    adjoint = jnp.concatenate([col_sin, col_cos], axis=0)
    inner_cos = row_cos[:, MARGIN : MARGIN + strip_rows]
    inner_sin = row_sin[:, MARGIN : MARGIN + strip_rows]
    mask_bf = jnp.tanh(phi).astype(jnp.bfloat16)
    window = padded_2(mask_bf, (("strip", 0),), MARGIN)
    spec_pair = product_t(window, forward).astype(jnp.bfloat16)
    cos_half = product(row_cos, spec_pair)
    sin_half = product(row_sin, spec_pair)
    s_re = scale_norm * (cos_half[:, :spectrum] + sin_half[:, spectrum:])
    s_im = scale_norm * (cos_half[:, spectrum:] - sin_half[:, :spectrum])
    middle = (LEVELS - 1) / 2.0
    defocus = (defocus_ids[0].astype(jnp.float32) - middle) / middle
    phase_turn = defocus * psi
    cos_turn = jnp.cos(phase_turn)
    sin_turn = jnp.sin(phase_turn)
    k_re = kernels[0] * cos_turn - kernels[1] * sin_turn
    k_im = kernels[0] * sin_turn + kernels[1] * cos_turn
    g_pair = jnp.concatenate([k_re * s_re - k_im * s_im, k_re * s_im + k_im * s_re], axis=2).astype(
        jnp.bfloat16
    )
    head_part = jnp.einsum("fr,kfc->krc", inner_cos, g_pair, preferred_element_type=jnp.float32)
    tail_part = jnp.einsum("fr,kfc->krc", inner_sin, g_pair, preferred_element_type=jnp.float32)
    q_re = head_part[..., :spectrum] - tail_part[..., spectrum:]
    q_im = head_part[..., spectrum:] + tail_part[..., :spectrum]
    q_pair = (
        jnp.concatenate([q_re, q_im], axis=2)
        .astype(jnp.bfloat16)
        .reshape(kernel_count * strip_rows, 2 * spectrum)
    )
    e_re = (scale_norm * product(q_pair, forward)).reshape(kernel_count, strip_rows, col_count)
    e_im = (scale_norm * product(q_pair, adjoint)).reshape(kernel_count, strip_rows, col_count)
    intensity = jnp.mean(e_re * e_re + e_im * e_im, axis=0)
    resist = jax.nn.sigmoid(slope_resist * (intensity - level_resist))
    weight = (
        4.0
        * slope_resist
        / kernel_count
        * (resist - target.astype(jnp.float32))
        * resist
        * (1.0 - resist)
    )
    v_re = (weight * e_re).astype(jnp.bfloat16).reshape(kernel_count * strip_rows, col_count)
    v_im = (weight * e_im).astype(jnp.bfloat16).reshape(kernel_count * strip_rows, col_count)
    u_pair = (
        (product_t(v_re, forward) + product_t(v_im, adjoint))
        .astype(jnp.bfloat16)
        .reshape(kernel_count, strip_rows, 2 * spectrum)
    )
    head_back = jnp.einsum("fr,krc->kfc", inner_cos, u_pair, preferred_element_type=jnp.float32)
    tail_back = jnp.einsum("fr,krc->kfc", inner_sin, u_pair, preferred_element_type=jnp.float32)
    w_re = scale_norm * (head_back[..., :spectrum] + tail_back[..., spectrum:])
    w_im = scale_norm * (head_back[..., spectrum:] - tail_back[..., :spectrum])
    y_re = jnp.sum(k_re * w_re + k_im * w_im, axis=0)
    y_im = jnp.sum(k_re * w_im - k_im * w_re, axis=0)
    y_re, y_im = (
        lax.psum(y_re.astype(jnp.bfloat16), "focus").astype(jnp.float32),
        lax.psum(y_im.astype(jnp.bfloat16), "focus").astype(jnp.float32),
    )
    stacked = jnp.stack([y_re, y_im])[None]
    beside_all = padded_2(stacked.astype(jnp.bfloat16), (("strip", 0),), 1).astype(stacked.dtype)
    own_rows = spectral_rows(inner_cos, inner_sin, y_re, y_im)
    prev_rows = spectral_rows(
        row_cos[:, MARGIN + strip_rows :],
        row_sin[:, MARGIN + strip_rows :],
        beside_all[0, 0],
        beside_all[0, 1],
    )
    next_rows = spectral_rows(
        row_cos[:, :MARGIN], row_sin[:, :MARGIN], beside_all[2, 0], beside_all[2, 1]
    )
    grad_rows = scale_norm * product(
        jnp.concatenate([own_rows, prev_rows, next_rows], axis=0), forward
    )
    folded = grad_rows[:strip_rows]
    folded = (
        folded.at[:MARGIN]
        .add(grad_rows[strip_rows : strip_rows + MARGIN])
        .at[strip_rows - MARGIN :]
        .add(grad_rows[strip_rows + MARGIN :])
    )
    mask_slope = 1.0 - jnp.tanh(phi) * jnp.tanh(phi)
    level_set = phi - step_size * mask_slope * folded
    for counter in range(SWEEPS):
        extended_set = padded_2(level_set.astype(jnp.bfloat16), (("strip", 0),), 1).astype(
            level_set.dtype
        )
        level_set = curvature_step(extended_set)
    return level_set


def solution(mesh):
    return jax.shard_map(
        on_device,
        mesh=mesh,
        in_specs=(
            P(("tile", "strip"), None),
            P(("tile", "strip"), None),
            P(("tile", "focus")),
            P(),
            P(),
            P(),
            P(),
        ),
        out_specs=P(("tile", "strip"), None),
        check_vma=False,
    )
```

profile of v0, /device:TPU:0, one launch (start us, length us, event | category | flops | bytes accessed | tf_op | source)
XLA Modules:
  0.0 140.7 jit_solution(1823749973720386125)
XLA Ops:
  6.5 1.1 tanh_convert_fusion
  7.7 0.0 copy-start.9
  7.7 1.3 collective-permute-start.1
  9.0 3.0 %collective-permute-start = (bf16[64,2048]{1,0:T(8,128)(2,1)S(1)}, bf16[64,2048]{1,0:T(8,128)(2,1)S(1)}, u32[]{:S(2)}, u32[]{:S(2)}) collective-permute-start(bf16[64,2048]{1,0:T(8,128)(2,1)S(1)} %tanh_convert_fusion), channel_id=1, source_target_pairs={{0,4},{4,8},{8,12},{1,5},{5,9},{9,13},{2,6},{6,10},{10,14},{3,7},{... | collective-permute-start | bytes 786440 | tf_op jit(solution)/shard_map/ppermute | solution.py:22
  12.0 18.9 %sine_convert_fusion = (bf16[512,2048]{1,0:T(8,128)(2,1)S(1)}, bf16[512,2048]{1,0:T(8,128)(2,1)S(1)}) fusion(s32[512]{0:T(512)} %param.21), kind=kLoop, calls=%fused_computation.8 | loop fusion | flops 16777216 | bytes 4196352 | tf_op jit(solution)/shard_map/convert_element_type | solution.py:34
  30.9 0.0 copy-start.10
  30.9 16.9 %fusion.22 = bf16[512,2048]{1,0:T(8,128)(2,1)S(1)} fusion(s32[512]{0:T(512)S(1)} %copy-done.9), kind=kLoop, calls=%fused_computation.50 | loop fusion | flops 18874368 | bytes 2099200 | tf_op jit(solution)/shard_map/neg | solution.py:90
  48.5 0.3 cosine_convert_fusion.1
  48.8 0.0 collective-permute-done.1
  48.8 0.0 collective-permute-done
  48.8 0.0 copy-start.8
  48.8 1.6 %convolution_convert_fusion = bf16[192,1024]{1,0:T(8,128)(2,1)S(1)} fusion(bf16[64,2048]{1,0:T(8,128)(2,1)S(1)} %collective-permute-done.1, bf16[64,2048]{1,0:T(8,128)(2,1)S(1)} %tanh_convert_fusion, bf16[64,2048]{1,0:T(8,128)(2,1)S(1)} %collective-permute-done, bf16[512,2048]{1,0:T(8,128)(2,1)S(1)} %fusion.22, bf16[512,2048]{1,0:T(8,128)(2,1)S(1)} %get-tuple-element.65), kind=kOutput, calls=%fused_computation.28 | convolution fusion | flops 816250880 | bytes 5373952 | tf_op jit(solution)/shard_map/dot_general | solution.py:42
  50.4 0.0 copy-start.7
  50.4 0.4 fusion.93
  50.8 0.4 fusion.92
  51.2 0.4 fusion.60
  51.6 0.2 subtract_convert_fusion
  51.8 0.1 add_convert_fusion.1
  51.9 0.4 convolution_bitcast_fusion
  52.3 0.4 convolution_bitcast_fusion.1
  52.7 0.3 fusion.43
  53.0 1.3 convolution_multiply_fusion.1
  54.3 3.0 %multiply_add_fusion = (f32[256,2048]{1,0:T(8,128)}, f32[256,2048]{1,0:T(8,128)}) fusion(f32[256,2048]{1,0:T(8,128)S(1)} %convolution_multiply_fusion.1, bf16[512,2048]{1,0:T(8,128)(2,1)S(1)} %get-tuple-element.65, bf16[512,2048]{1,0:T(8,128)(2,1)S(1)} %get-tuple-element.64, bf16[256,512]{1,0:T(8,128)(2,1)S(1)} %bitcast.84, bf16[256,512]{1,0:T(8,128)(2,1)S(1)} %bitcast.82), kind=kOutput, calls=%fused_computation.21 | convolution fusion | flops 1085276160 | bytes 11010048 | tf_op jit(solution)/shard_map/dot_general | solution.py:38
  57.3 1.8 %reduce_sum.27 = f32[64,2048]{1,0:T(8,128)S(1)} reduce(f32[4,64,2048]{2,1,0:T(8,128)} %bitcast.76, f32[]{:T(128)} %constant.126.clone.1), dimensions={0}, to_apply=%region_0.1 | reduce | flops 393216 | bytes 2621444 | tf_op jit(solution)/shard_map/reduce_sum | solution.py:122
  59.1 1.3 subtract_multiply_fusion
  60.3 2.9 %fusion.8 = (bf16[256,2048]{1,0:T(8,128)(2,1)S(1)}, bf16[256,2048]{1,0:T(8,128)(2,1)S(1)}) fusion(f32[256,2048]{1,0:T(8,128)} %get-tuple-element.69, f32[64,2048]{1,0:T(8,128)S(1)} %subtract_multiply_fusion, f32[256,2048]{1,0:T(8,128)} %copy-done), kind=kLoop, calls=%fused_computation.20 | loop fusion | flops 2097152 | bytes 6815744 | tf_op jit(solution)/shard_map/convert_element_type | solution.py:133
  63.3 1.3 fusion.107
  64.6 0.3 copy-done.5
  64.9 1.3 fusion.10
  66.2 0.3 convolution_bitcast_fusion.3
  66.5 0.3 convolution_bitcast_fusion.2
  66.8 0.9 add_reduce_fusion
  67.7 0.0 all-reduce.5.cloned.1.call-update
  67.7 37.2 %all-reduce.5.cloned.1.call-done = (bf16[48,512]{1,0:T(8,128)(2,1)}, bf16[48,512]{1,0:T(8,128)(2,1)}) async-done(((bf16[48,512]{1,0:T(8,128)(2,1)}, bf16[48,512]{1,0:T(8,128)(2,1)}), (bf16[48,512]{1,0:T(8,128)(2,1)}, bf16[48,512]{1,0:T(8,128)(2,1)})) %all-reduce.5.cloned.1.call-update) | async-done | bytes 98320 | tf_op jit(solution)/shard_map/psum | solution.py:147
  104.9 1.0 pad_maximum_fusion.14
  105.9 1.3 collective-permute-start.3
  107.2 3.2 %collective-permute-start.2 = (bf16[1,2,48,512]{3,2,1,0:T(8,128)(2,1)S(1)}, bf16[1,2,48,512]{3,2,1,0:T(8,128)(2,1)S(1)}, u32[]{:S(2)}, u32[]{:S(2)}) collective-permute-start(bf16[1,2,48,512]{3,2,1,0:T(8,128)(2,1)S(1)} %pad_maximum_fusion.14), channel_id=1, source_target_pairs={{0,4},{4,8},{8,12},{1,5},{5,9},{9,13},{2,6},{6,10},{10,14},{3,7},{... | collective-permute-start | bytes 294920 | tf_op jit(solution)/shard_map/ppermute | solution.py:22
  110.4 1.0 fusion.89
  111.5 1.0 fusion.87
  112.6 1.1 fusion.12
  113.6 1.1 fusion.11
  114.7 0.0 collective-permute-done.2
  114.7 0.2 fusion.66
  114.9 0.2 fusion.67
  115.1 0.2 fusion.68
  115.3 0.2 fusion.69
  115.4 0.2 fusion.14
  115.6 0.2 fusion.13
  115.8 0.2 fusion.16
  116.0 0.2 fusion.15
  116.2 0.0 copy-start.6
  116.2 1.0 convolution_multiply_fusion.2
  117.3 0.2 fusion.41
  117.5 3.0 %collective-permute-start.4 = (bf16[1,2048]{1,0:T(2,128)(2,1)S(1)}, bf16[1,2048]{1,0:T(2,128)(2,1)S(1)}, u32[]{:S(2)}, u32[]{:S(2)}) collective-permute-start(bf16[1,2048]{1,0:T(2,128)(2,1)S(1)} %get-tuple-element.60), channel_id=1, source_target_pairs={{0,4},{4,8},{8,12},{1,5},{5,9},{9,13},{2,6},{6,10},{10,14},{3,7},{... | collective-permute-start | bytes 12296 | tf_op jit(solution)/shard_map/ppermute | solution.py:22
  120.5 1.3 collective-permute-start.5
  121.8 0.0 collective-permute-done.4
  121.8 1.8 %collective-permute-done.5 = bf16[1,2048]{1,0:T(2,128)(2,1)S(1)} collective-permute-done((bf16[1,2048]{1,0:T(2,128)(2,1)S(1)}, bf16[1,2048]{1,0:T(2,128)(2,1)S(1)}, u32[]{:S(2)}, u32[]{:S(2)}) %collective-permute-start.5) | collective-permute-done | bytes 4128 | tf_op jit(solution)/shard_map/ppermute | solution.py:25
  123.5 0.1 maximum_convert_fusion
  123.6 1.0 add_convert_fusion
  124.6 4.3 %collective-permute-start.6 = (bf16[1,2048]{1,0:T(2,128)(2,1)S(1)}, bf16[1,2048]{1,0:T(2,128)(2,1)S(1)}, u32[]{:S(2)}, u32[]{:S(2)}) collective-permute-start(bf16[1,2048]{1,0:T(2,128)(2,1)S(1)} %get-tuple-element.58), channel_id=1, source_target_pairs={{0,4},{4,8},{8,12},{1,5},{5,9},{9,13},{2,6},{6,10},{10,14},{3,7},{... | collective-permute-start | bytes 12296 | tf_op jit(solution)/shard_map/ppermute | solution.py:22
  129.0 1.3 collective-permute-start.7
  130.3 1.8 %collective-permute-done.7 = bf16[1,2048]{1,0:T(2,128)(2,1)S(1)} collective-permute-done((bf16[1,2048]{1,0:T(2,128)(2,1)S(1)}, bf16[1,2048]{1,0:T(2,128)(2,1)S(1)}, u32[]{:S(2)}, u32[]{:S(2)}) %collective-permute-start.7) | collective-permute-done | bytes 4128 | tf_op jit(solution)/shard_map/ppermute | solution.py:25
  132.0 0.1 maximum_convert_fusion.1
  132.1 1.8 %multiply_add_fusion.1 = f32[64,2048]{1,0:T(8,128)} fusion(f32[66,2048]{1,0:T(8,128)S(1)} %maximum_convert_fusion.1), kind=kLoop, calls=%fused_computation.89 | loop fusion | flops 3670016 | bytes 2686976 | tf_op jit(solution)/shard_map/add | solution.py:79
  (21 shorter events, 0.1 us)
Async XLA Ops:
  6.5 98.4 %all-reduce.5.cloned.1.call-start = ((), (), s32[]{:S(2)}) async-start(), calls=%async_computation | async-start | bytes 196608 | tf_op jit(solution)/shard_map/psum | solution.py:147
  7.7 23.2 %copy-start.9 = (s32[512]{0:T(512)S(1)}, s32[512]{0:T(512)}, u32[]{:S(2)}) copy-start(s32[512]{0:T(512)} %param.21) | copy-start | bytes 6148
  7.7 41.1 %collective-permute-start.1 = (bf16[64,2048]{1,0:T(8,128)(2,1)S(1)}, bf16[64,2048]{1,0:T(8,128)(2,1)S(1)}, u32[]{:S(2)}, u32[]{:S(2)}) collective-permute-start(bf16[64,2048]{1,0:T(8,128)(2,1)S(1)} %tanh_convert_fusion), channel_id=1, source_target_pairs={{4,0},{8,4},{12,8},{5,1},{9,5},{13,9},{6,2},{10,6},{14,10},{7,3},{... | collective-permute-start | bytes 786440 | tf_op jit(solution)/shard_map/ppermute | solution.py:25
  9.0 39.9 %collective-permute-start = (bf16[64,2048]{1,0:T(8,128)(2,1)S(1)}, bf16[64,2048]{1,0:T(8,128)(2,1)S(1)}, u32[]{:S(2)}, u32[]{:S(2)}) collective-permute-start(bf16[64,2048]{1,0:T(8,128)(2,1)S(1)} %tanh_convert_fusion), channel_id=1, source_target_pairs={{0,4},{4,8},{8,12},{1,5},{5,9},{9,13},{2,6},{6,10},{10,14},{3,7},{... | collective-permute-start | bytes 786440 | tf_op jit(solution)/shard_map/ppermute | solution.py:22
  30.9 23.4 %copy-start.1 = (bf16[512,2048]{1,0:T(8,128)(2,1)}, bf16[512,2048]{1,0:T(8,128)(2,1)S(1)}, u32[]{:S(2)}) copy-start(bf16[512,2048]{1,0:T(8,128)(2,1)S(1)} %get-tuple-element.65) | copy-start | bytes 6291460
  30.9 23.4 %copy-start.4 = (bf16[512,2048]{1,0:T(8,128)(2,1)}, bf16[512,2048]{1,0:T(8,128)(2,1)S(1)}, u32[]{:S(2)}) copy-start(bf16[512,2048]{1,0:T(8,128)(2,1)S(1)} %get-tuple-element.64) | copy-start | bytes 6291460
  30.9 17.6 %copy-start.10 = (s32[48]{0:T(128)S(1)}, s32[48]{0:T(128)}, u32[]{:S(2)}) copy-start(s32[48]{0:T(128)} %param.20) | copy-start | bytes 580
  48.8 2.4 %copy-start.8 = (f32[48,512]{1,0:T(8,128)S(1)}, f32[48,512]{1,0:T(8,128)}, u32[]{:S(2)}) copy-start(f32[48,512]{1,0:T(8,128)} %param.19) | copy-start | bytes 294916
  50.4 1.2 copy-start.7
  54.3 3.0 %copy-start = (f32[256,2048]{1,0:T(8,128)}, f32[256,2048]{1,0:T(8,128)S(1)}, u32[]{:S(2)}) copy-start(f32[256,2048]{1,0:T(8,128)S(1)} %convolution_multiply_fusion.1) | copy-start | bytes 6291460
  60.3 2.9 %copy-start.2 = (bf16[512,2048]{1,0:T(8,128)(2,1)S(1)}, bf16[512,2048]{1,0:T(8,128)(2,1)}, u32[]{:S(2)}) copy-start(bf16[512,2048]{1,0:T(8,128)(2,1)} %copy-done.1) | copy-start | bytes 6291460
  63.3 1.6 %copy-start.5 = (bf16[512,2048]{1,0:T(8,128)(2,1)S(1)}, bf16[512,2048]{1,0:T(8,128)(2,1)}, u32[]{:S(2)}) copy-start(bf16[512,2048]{1,0:T(8,128)(2,1)} %copy-done.4) | copy-start | bytes 6291460
  104.9 11.3 %copy-start.3 = (bf16[512,2048]{1,0:T(8,128)(2,1)S(1)}, bf16[512,2048]{1,0:T(8,128)(2,1)}, u32[]{:S(2)}) copy-start(bf16[512,2048]{1,0:T(8,128)(2,1)} %copy-done.1) | copy-start | bytes 6291460
  105.9 9.1 %collective-permute-start.3 = (bf16[1,2,48,512]{3,2,1,0:T(8,128)(2,1)S(1)}, bf16[1,2,48,512]{3,2,1,0:T(8,128)(2,1)S(1)}, u32[]{:S(2)}, u32[]{:S(2)}) collective-permute-start(bf16[1,2,48,512]{3,2,1,0:T(8,128)(2,1)S(1)} %pad_maximum_fusion.14), channel_id=1, source_target_pairs={{4,0},{8,4},{12,8},{5,1},{9,5},{13,9},{6,2},{10,6},{14,10},{7,3},{... | collective-permute-start | bytes 294920 | tf_op jit(solution)/shard_map/ppermute | solution.py:25
  107.2 7.5 %collective-permute-start.2 = (bf16[1,2,48,512]{3,2,1,0:T(8,128)(2,1)S(1)}, bf16[1,2,48,512]{3,2,1,0:T(8,128)(2,1)S(1)}, u32[]{:S(2)}, u32[]{:S(2)}) collective-permute-start(bf16[1,2,48,512]{3,2,1,0:T(8,128)(2,1)S(1)} %pad_maximum_fusion.14), channel_id=1, source_target_pairs={{0,4},{4,8},{8,12},{1,5},{5,9},{9,13},{2,6},{6,10},{10,14},{3,7},{... | collective-permute-start | bytes 294920 | tf_op jit(solution)/shard_map/ppermute | solution.py:22
  116.2 1.1 copy-start.6
  117.5 4.3 %collective-permute-start.4 = (bf16[1,2048]{1,0:T(2,128)(2,1)S(1)}, bf16[1,2048]{1,0:T(2,128)(2,1)S(1)}, u32[]{:S(2)}, u32[]{:S(2)}) collective-permute-start(bf16[1,2048]{1,0:T(2,128)(2,1)S(1)} %get-tuple-element.60), channel_id=1, source_target_pairs={{0,4},{4,8},{8,12},{1,5},{5,9},{9,13},{2,6},{6,10},{10,14},{3,7},{... | collective-permute-start | bytes 12296 | tf_op jit(solution)/shard_map/ppermute | solution.py:22
  120.5 3.1 %collective-permute-start.5 = (bf16[1,2048]{1,0:T(2,128)(2,1)S(1)}, bf16[1,2048]{1,0:T(2,128)(2,1)S(1)}, u32[]{:S(2)}, u32[]{:S(2)}) collective-permute-start(bf16[1,2048]{1,0:T(2,128)(2,1)S(1)} %get-tuple-element.61), channel_id=1, source_target_pairs={{4,0},{8,4},{12,8},{5,1},{9,5},{13,9},{6,2},{10,6},{14,10},{7,3},{... | collective-permute-start | bytes 12296 | tf_op jit(solution)/shard_map/ppermute | solution.py:25
  124.6 5.6 %collective-permute-start.6 = (bf16[1,2048]{1,0:T(2,128)(2,1)S(1)}, bf16[1,2048]{1,0:T(2,128)(2,1)S(1)}, u32[]{:S(2)}, u32[]{:S(2)}) collective-permute-start(bf16[1,2048]{1,0:T(2,128)(2,1)S(1)} %get-tuple-element.58), channel_id=1, source_target_pairs={{0,4},{4,8},{8,12},{1,5},{5,9},{9,13},{2,6},{6,10},{10,14},{3,7},{... | collective-permute-start | bytes 12296 | tf_op jit(solution)/shard_map/ppermute | solution.py:22
  129.0 3.1 %collective-permute-start.7 = (bf16[1,2048]{1,0:T(2,128)(2,1)S(1)}, bf16[1,2048]{1,0:T(2,128)(2,1)S(1)}, u32[]{:S(2)}, u32[]{:S(2)}) collective-permute-start(bf16[1,2048]{1,0:T(2,128)(2,1)S(1)} %get-tuple-element.59), channel_id=1, source_target_pairs={{4,0},{8,4},{12,8},{5,1},{9,5},{13,9},{6,2},{10,6},{14,10},{7,3},{... | collective-permute-start | bytes 12296 | tf_op jit(solution)/shard_map/ppermute | solution.py:25
Sparse Core Ops, SparseCore 0:
  67.8 37.0 all-reduce.4
where the time goes:
time: 143 us; the launch traced here: 141 us
  other arithmetic  49 us (34%)
  waiting for transfers between devices  40.8 us (29%)
  starting transfers between devices  18.7 us (13%)
  matrix products  17.2 us (12%)
  between operations  14.6 us (10%)
    psum x1, waiting for transfers between devices, on_device(): lax.psum(y_im.astype(jnp.bfloat16), 'focus').astype(jnp.float32)  37.2 us
    convert_element_type x1, other arithmetic, tables(): jnp.sin(angles).astype(jnp.bfloat16)  18.9 us
    neg x1, other arithmetic, on_device(): forward = jnp.concatenate([col_cos, -col_sin], axis=0)  16.9 us
    ppermute x4, starting transfers between devices, padded_2(): lax.ppermute(lax.slice_in_dim(block, block.shape[dim] - width, None, axis...  13.5 us
    dot_general x5, matrix products, product(): return jnp.dot(lhs_mat, rhs_mat, preferred_element_type=jnp.float32)  6.07 us
    dot_general x12, matrix products, exact_t(): lax.dot_general(lhs_mat.astype(jnp.float32), rhs_mat, (((0,), (0,)), ((),...  5.64 us
    ppermute x4, starting transfers between devices, padded_2(): lax.ppermute(lax.slice_in_dim(block, 0, width, axis=dim), axis, backward)  5.17 us
    dot_general x3, matrix products, product_t(): lax.dot_general(lhs_mat, rhs_mat, (((1,), (1,)), ((), ())), preferred_ele...  4.11 us
  transfers between devices with their start and end apart: 9, of which 3 were waited for; matrix products, arithmetic and copies ran while one was open for 29% of the time, Pallas kernels for 0%

commit v1 on v0

v1 whole, which is shorter than its diff:
```python
import functools

import jax
import jax.numpy as jnp
from jax import lax
from jax.experimental import pallas as pl
from jax.experimental.pallas import tpu as pltpu
from jax.sharding import PartitionSpec as P

MARGIN = 64
LEVELS = 31
SWEEPS = 2
HALO = 8
LANES = 128
OFFSETS = (-2, -1, 1, 2)
MESH = pl.DeviceIdType.MESH

slope_resist = 4.0
level_resist = 0.5
step_size = 1.0
flow_rate = 0.2

SIN_TERMS = (1.0, -1.0 / 6.0, 1.0 / 120.0, -1.0 / 5040.0, 1.0 / 362880.0)
COS_TERMS = (1.0, -0.5, 1.0 / 24.0, -1.0 / 720.0, 1.0 / 40320.0)


def series(terms, square):
    total = jnp.full_like(square, terms[-1])
    for term in terms[-2::-1]:
        total = total * square + term
    return total


def turn_pair(turns):
    quarter = jnp.floor(4.0 * turns + 0.5)
    angle = (turns - 0.25 * quarter) * (2.0 * jnp.pi)
    square = angle * angle
    cos_0 = series(COS_TERMS, square)
    sin_0 = angle * series(SIN_TERMS, square)
    kind = quarter.astype(jnp.int32) & 3
    odd = (kind & 1) == 1
    cos_1 = jnp.where(odd, sin_0, cos_0)
    sin_1 = jnp.where(odd, cos_0, sin_0)
    cos_out = jnp.where((kind == 1) | (kind == 2), -cos_1, cos_1)
    sin_out = jnp.where(kind >= 2, -sin_1, sin_1)
    return cos_out, sin_out


def whole_turns(steps, period):
    return (steps - period * jnp.floor(steps * (1.0 / period) + 0.5)) * (1.0 / period)


def dot(lhs, rhs):
    return jnp.dot(lhs, rhs, preferred_element_type=jnp.float32)


def dot_t(lhs, rhs):
    return lax.dot_general(
        lhs, rhs, (((1,), (1,)), ((), ())), preferred_element_type=jnp.float32
    )


def iota(shape, dim):
    return lax.broadcasted_iota(jnp.int32, shape, dim)


def kernel(
    strips,
    planes,
    freqs_ref,
    defocus_ref,
    phi_ref,
    target_ref,
    kernels_ref,
    psi_ref,
    out_ref,
    table,
    freq_col,
    window,
    halo,
    k_re,
    k_im,
    spec,
    q_ref,
    v_ref,
    row_out,
    row_in,
    y_send,
    y_recv,
    y_sum,
    y_side,
    z_ref,
    grad,
    mask_send,
    mask_recv,
    halo_send,
    halo_recv,
    rs_send,
    rs_recv,
    side_send,
    side_recv,
    ag_send,
    ag_recv,
):
    rows, cols = phi_ref.shape
    kern, fr, fc = kernels_ref.shape[1:]
    chunks, _, wide = y_send.shape
    stride = planes // chunks
    win = rows + 2 * MARGIN
    ext = rows + 2 * HALO
    both = 2 * fr
    norm = float((win * cols) ** -0.5)
    bf16 = jnp.bfloat16
    strip = lax.axis_index("strip")
    focus = lax.axis_index("focus")

    def inside(offset):
        place = strip + offset
        return jnp.logical_and(place >= 0, place < strips)

    def to_strip(src, dst, send, recv, offset):
        return pltpu.make_async_remote_copy(
            src_ref=src,
            dst_ref=dst,
            send_sem=send,
            recv_sem=recv,
            device_id={"strip": strip + offset},
            device_id_type=MESH,
        )

    def to_focus(src, dst, send, recv, peer):
        return pltpu.make_async_remote_copy(
            src_ref=src,
            dst_ref=dst,
            send_sem=send,
            recv_sem=recv,
            device_id={"focus": peer},
            device_id_type=MESH,
        )

    barrier = pltpu.get_barrier_semaphore()
    for offset in OFFSETS:

        @pl.when(inside(offset))
        def _(offset=offset):
            pl.semaphore_signal(
                barrier, inc=1, device_id={"strip": strip + offset}, device_id_type=MESH
            )

    for step in range(1, planes):
        pl.semaphore_signal(
            barrier,
            inc=1,
            device_id={"focus": lax.rem(focus + step, planes)},
            device_id_type=MESH,
        )

    window[MARGIN : MARGIN + rows, :] = jnp.tanh(phi_ref[...]).astype(bf16)

    beside = jnp.minimum(strip, 2) + jnp.minimum(strips - 1 - strip, 2)
    pl.semaphore_wait(barrier, planes - 1 + beside)

    def mask_copy(offset):
        if offset == 1:
            src, dst, slot = window.at[rows : rows + MARGIN], window.at[:MARGIN], 0
        else:
            src, dst, slot = window.at[MARGIN : 2 * MARGIN], window.at[MARGIN + rows :], 1
        return to_strip(src, dst, mask_send.at[slot], mask_recv.at[slot], offset)

    def halo_copy(offset):
        if offset == 1:
            src, slot = phi_ref.at[rows - HALO :], 0
        else:
            src, slot = phi_ref.at[:HALO], 1
        return to_strip(src, halo.at[slot], halo_send.at[slot], halo_recv.at[slot], offset)

    for copy in (mask_copy, halo_copy):
        for offset in (1, -1):

            @pl.when(inside(offset))
            def _(copy=copy, offset=offset):
                copy(offset).start()

    for block in range(fc // LANES):
        lane_freqs = freqs_ref[:, block * LANES : (block + 1) * LANES]
        freq_col[block * LANES : (block + 1) * LANES, :] = jnp.broadcast_to(
            lane_freqs, (LANES, LANES)
        ).T
    group = 32
    for chunk in range(chunks):

        @pl.loop(0, wide // group)
        def _(step, chunk=chunk):
            first = pl.multiple_of(step * group, group)
            freq = freq_col[pl.ds(chunk * wide + first, group), :]
            lane = iota((group, LANES), 1).astype(jnp.float32)
            cos_now, sin_now = turn_pair(whole_turns(freq * lane, float(cols)))
            cos_turn, sin_turn = turn_pair(whole_turns(freq * float(LANES), float(cols)))
            for part in range(cols // LANES):
                here = slice(part * LANES, (part + 1) * LANES)
                table[pl.ds(2 * chunk * wide + first, group), here] = cos_now.astype(bf16)
                table[pl.ds((2 * chunk + 1) * wide + first, group), here] = sin_now.astype(bf16)
                cos_now, sin_now = (
                    cos_now * cos_turn - sin_now * sin_turn,
                    sin_now * cos_turn + cos_now * sin_turn,
                )

    row_lane = freqs_ref[:, fc : fc + LANES]
    row_sub = jnp.broadcast_to(row_lane, (LANES, LANES)).T[:both, :1]
    row_lane = row_lane[:, :both]

    def row_cosine(freq, place, quarters):
        turns = whole_turns(freq * place.astype(jnp.float32), float(win))
        return turn_pair(turns + 0.25 * quarters.astype(jnp.float32))[0]

    shape = (both, win)
    row_all = row_cosine(
        jnp.broadcast_to(row_sub, shape), iota(shape, 1), -(iota(shape, 0) // fr)
    ).astype(bf16)
    shape = (both, 2 * rows)
    row_in[...] = row_cosine(
        jnp.broadcast_to(row_sub, shape),
        MARGIN + iota(shape, 1) % rows,
        iota(shape, 0) // fr - iota(shape, 1) // rows,
    ).astype(bf16)
    shape = (2 * rows, both)
    row_back = row_cosine(
        jnp.broadcast_to(row_lane, shape),
        MARGIN + iota(shape, 0) % rows,
        iota(shape, 1) // fr - iota(shape, 0) // rows,
    ).astype(bf16)

    middle = (LEVELS - 1) / 2.0
    defocus = (defocus_ref[0].astype(jnp.float32) - middle) * (1.0 / middle)
    cos_turn, sin_turn = turn_pair(psi_ref[...] * (defocus * (0.5 / jnp.pi)))
    for k in range(kern):
        best_re, best_im = kernels_ref[0, k], kernels_ref[1, k]
        full_re = best_re * cos_turn - best_im * sin_turn
        full_im = best_re * sin_turn + best_im * cos_turn
        for chunk in range(chunks):
            k_re[k, chunk] = full_re[:, chunk * wide : (chunk + 1) * wide]
            k_im[k, chunk] = full_im[:, chunk * wide : (chunk + 1) * wide]

    for offset, copy, spot in ((-1, 1, slice(0, MARGIN)), (1, -1, slice(MARGIN + rows, win))):

        @pl.when(inside(offset))
        def _(copy=copy):
            mask_copy(copy).wait_recv()

        @pl.when(jnp.logical_not(inside(offset)))
        def _(spot=spot):
            window[spot, :] = jnp.zeros((MARGIN, cols), bf16)

    @pl.loop(0, chunks)
    def _(chunk):
        here = pl.ds(pl.multiple_of(chunk * 2 * wide, 2 * wide), 2 * wide)
        spec[:, here] = dot_t(window[...], table[here, :]).astype(bf16)

    halves = dot(row_all, spec[...])
    for k in range(kern):
        tops, lows = [], []
        for chunk in range(chunks):
            at_cos = slice(2 * chunk * wide, (2 * chunk + 1) * wide)
            at_sin = slice((2 * chunk + 1) * wide, (2 * chunk + 2) * wide)
            s_re = norm * (halves[:fr, at_cos] - halves[fr:, at_sin])
            s_im = -norm * (halves[:fr, at_sin] + halves[fr:, at_cos])
            tops.append(k_re[k, chunk] * s_re - k_im[k, chunk] * s_im)
            lows.append(k_re[k, chunk] * s_im + k_im[k, chunk] * s_re)
        g_pair = jnp.concatenate(
            [jnp.concatenate(tops, axis=1), jnp.concatenate(lows, axis=1)], axis=0
        ).astype(bf16)
        q_pair = dot(row_back, g_pair)
        own = slice(k * rows, (k + 1) * rows)
        turned = slice((kern + k) * rows, (kern + k + 1) * rows)
        for chunk in range(chunks):
            at_cos = slice(2 * chunk * wide, (2 * chunk + 1) * wide)
            at_sin = slice((2 * chunk + 1) * wide, (2 * chunk + 2) * wide)
            q_re = q_pair[:rows, chunk * wide : (chunk + 1) * wide].astype(bf16)
            q_im = q_pair[rows:, chunk * wide : (chunk + 1) * wide].astype(bf16)
            q_ref[own, at_cos] = q_re
            q_ref[own, at_sin] = -q_im
            q_ref[turned, at_cos] = q_im
            q_ref[turned, at_sin] = q_re

    piece = 256

    @pl.loop(0, cols // piece)
    def _(step):
        here = pl.ds(pl.multiple_of(step * piece, piece), piece)
        field = dot(q_ref[...], table[:, here]).reshape(2 * kern, rows, piece)
        intensity = (norm * norm / kern) * jnp.sum(field * field, axis=0)
        resist = 1.0 / (1.0 + jnp.exp(-slope_resist * (intensity - level_resist)))
        weight = (
            (norm * 4.0 * slope_resist / kern)
            * (resist - target_ref[:, here].astype(jnp.float32))
            * resist
            * (1.0 - resist)
        )
        v_ref[:, here] = (field * weight[None]).reshape(2 * kern * rows, piece).astype(bf16)

    half = kern * rows

    def adjoint(chunk):
        here = pl.ds(pl.multiple_of(chunk * 2 * wide, 2 * wide), 2 * wide)
        u_all = dot_t(v_ref[...], table[here, :])
        u_re = (u_all[:half, :wide] + u_all[half:, wide:]).astype(bf16)
        u_im = (u_all[half:, :wide] - u_all[:half, wide:]).astype(bf16)
        stacked = jnp.concatenate(
            [
                jnp.concatenate(
                    [u_re[k * rows : (k + 1) * rows], u_im[k * rows : (k + 1) * rows]], axis=0
                )
                for k in range(kern)
            ],
            axis=1,
        )
        w_all = norm * dot(row_in[...], stacked)
        y_re = jnp.zeros((fr, wide), jnp.float32)
        y_im = jnp.zeros((fr, wide), jnp.float32)
        for k in range(kern):
            w_re = w_all[:fr, k * wide : (k + 1) * wide]
            w_im = w_all[fr:, k * wide : (k + 1) * wide]
            y_re += k_re[k, chunk] * w_re + k_im[k, chunk] * w_im
            y_im += k_re[k, chunk] * w_im - k_im[k, chunk] * w_re
        y_send[chunk] = jnp.concatenate([y_re, y_im], axis=0).astype(bf16)

    def to_owner(chunk):
        return to_focus(
            y_send.at[chunk],
            y_recv.at[focus],
            rs_send.at[chunk],
            rs_recv.at[focus],
            chunk * stride,
        )

    mine = focus // stride
    owner = lax.rem(focus, stride) == 0
    for step in list(range(1, chunks)) + [0]:
        chunk = lax.rem(mine + step, chunks)
        adjoint(chunk)
        if step:
            to_owner(chunk).start()
        elif stride > 1:

            @pl.when(jnp.logical_not(owner))
            def _(chunk=chunk):
                to_owner(chunk).start()

    shape = (2 * ext, both)
    for index, offset in enumerate((0,) + OFFSETS):
        place = iota(shape, 0) % ext - HALO - offset * rows + MARGIN
        values = row_cosine(
            jnp.broadcast_to(row_lane, shape),
            place,
            iota(shape, 1) // fr - iota(shape, 0) // ext,
        )
        covered = jnp.logical_and(place >= 0, place < win)
        row_out[index] = jnp.where(covered, values, 0.0).astype(bf16)

    def side_copy(offset):
        slot = OFFSETS.index(-offset)
        return to_strip(y_sum, y_side.at[slot], side_send.at[slot], side_recv.at[slot], offset)

    def gather_copy(step):
        peer = lax.rem(focus + step, planes)
        return to_focus(z_ref.at[mine], z_ref.at[mine], ag_send.at[step], ag_recv.at[mine], peer)

    def own_part():
        total = y_send[mine].astype(jnp.float32)
        for step in range(1, planes):
            source = lax.rem(focus + step, planes)
            to_focus(
                y_send.at[0], y_recv.at[source], rs_send.at[0], rs_recv.at[source], source
            ).wait_recv()
            total += y_recv[source].astype(jnp.float32)
        y_sum[...] = total.astype(bf16)
        for offset in OFFSETS:

            @pl.when(inside(offset))
            def _(offset=offset):
                side_copy(offset).start()

        rows_z = dot(row_out[0], y_sum[...])
        for index, offset in enumerate(OFFSETS):

            @pl.when(inside(offset))
            def _(offset=offset):
                side_copy(-offset).wait_recv()

            @pl.when(jnp.logical_not(inside(offset)))
            def _(index=index):
                y_side[index] = jnp.zeros((both, wide), bf16)

            rows_z += dot(row_out[index + 1], y_side[index])
        z_ref[mine] = jnp.concatenate([rows_z[:ext], -rows_z[ext:]], axis=1).astype(bf16)
        for step in range(1, planes):
            gather_copy(step).start()

    if stride > 1:
        pl.when(owner)(own_part)
    else:
        own_part()

    def part_grad(chunk):
        here = pl.ds(pl.multiple_of(chunk * 2 * wide, 2 * wide), 2 * wide)
        return dot(z_ref[chunk], table[here, :])

    for step in range(chunks):
        chunk = lax.rem(mine + step, chunks)
        if step:
            to_focus(
                z_ref.at[chunk], z_ref.at[chunk], ag_send.at[0], ag_recv.at[chunk], chunk * stride
            ).wait_recv()
            grad[...] += part_grad(chunk)
        else:
            if stride > 1:

                @pl.when(jnp.logical_not(owner))
                def _(chunk=chunk):
                    to_focus(
                        z_ref.at[chunk],
                        z_ref.at[chunk],
                        ag_send.at[0],
                        ag_recv.at[chunk],
                        chunk * stride,
                    ).wait_recv()

            grad[...] = part_grad(chunk)

    for index, offset in enumerate((-1, 1)):

        @pl.when(inside(offset))
        def _(offset=offset):
            halo_copy(-offset).wait_recv()

        @pl.when(jnp.logical_not(inside(offset)))
        def _(index=index):
            halo[index] = jnp.zeros((HALO, cols), jnp.float32)

    level = jnp.concatenate([halo[0], phi_ref[...], halo[1]], axis=0)
    slope = jnp.tanh(level)
    row_place = strip * rows + iota((ext, cols), 0) - HALO
    in_tile = jnp.logical_and(row_place >= 0, row_place < strips * rows)
    level = level - (step_size * norm) * (1.0 - slope * slope) * grad[...]
    level = jnp.where(in_tile, level, 0.0)
    column = iota((ext, cols), 1)
    for sweep in range(SWEEPS):
        right = jnp.where(column == cols - 1, 0.0, pltpu.roll(level, cols - 1, 1))
        left = jnp.where(column == 0, 0.0, pltpu.roll(level, 1, 1))
        across = right - left
        upper = pltpu.roll(level, ext - 1, 0)
        lower = pltpu.roll(level, 1, 0)
        diagonal = pltpu.roll(across, ext - 1, 0) - pltpu.roll(across, 1, 0)
        grad_x = 0.5 * (upper - lower)
        grad_y = 0.5 * across
        second_x = upper - 2.0 * level + lower
        second_y = right - 2.0 * level + left
        cross = 0.25 * diagonal
        flow = (
            second_x * grad_y * grad_y - 2.0 * grad_x * grad_y * cross + second_y * grad_x * grad_x
        ) / (1.0 + grad_x * grad_x + grad_y * grad_y)
        level = jnp.where(in_tile, level + flow_rate * flow, 0.0)
    out_ref[...] = level[HALO : HALO + rows]

    for copy in (mask_copy, halo_copy):
        for offset in (1, -1):

            @pl.when(inside(offset))
            def _(copy=copy, offset=offset):
                copy(offset).wait_send()

    for step in range(chunks):
        chunk = lax.rem(mine + step, chunks)
        if step:
            to_owner(chunk).wait_send()
        elif stride > 1:

            @pl.when(jnp.logical_not(owner))
            def _(chunk=chunk):
                to_owner(chunk).wait_send()

    def own_sent():
        for offset in OFFSETS:

            @pl.when(inside(offset))
            def _(offset=offset):
                side_copy(offset).wait_send()

        for step in range(1, planes):
            gather_copy(step).wait_send()

    if stride > 1:
        pl.when(owner)(own_sent)
    else:
        own_sent()


def on_device(strips, planes, phi, target, defocus_ids, kernels, psi, row_freqs, col_freqs):
    rows, cols = phi.shape
    _, kern, fr, fc = kernels.shape
    wide = max(LANES, fc // planes)
    chunks = fc // wide
    ext = rows + 2 * HALO
    win = rows + 2 * MARGIN
    filler = jnp.zeros((LANES - 2 * fr,), jnp.int32)
    freqs = jnp.concatenate([col_freqs, row_freqs, row_freqs, filler]).astype(jnp.float32)[None]
    vmem = pl.BlockSpec(memory_space=pltpu.VMEM)
    smem = pl.BlockSpec(memory_space=pltpu.SMEM)
    bf16, f32 = jnp.bfloat16, jnp.float32
    return pl.pallas_call(
        functools.partial(kernel, strips, planes),
        out_shape=jax.ShapeDtypeStruct((rows, cols), f32),
        in_specs=[vmem, smem, vmem, vmem, vmem, vmem],
        out_specs=vmem,
        scratch_shapes=[
            pltpu.VMEM((2 * fc, cols), bf16),
            pltpu.VMEM((fc, LANES), f32),
            pltpu.VMEM((win, cols), bf16),
            pltpu.VMEM((2, HALO, cols), f32),
            pltpu.VMEM((kern, chunks, fr, wide), f32),
            pltpu.VMEM((kern, chunks, fr, wide), f32),
            pltpu.VMEM((win, 2 * fc), bf16),
            pltpu.VMEM((2 * kern * rows, 2 * fc), bf16),
            pltpu.VMEM((2 * kern * rows, cols), bf16),
            pltpu.VMEM((1 + len(OFFSETS), 2 * ext, 2 * fr), bf16),
            pltpu.VMEM((2 * fr, 2 * rows), bf16),
            pltpu.VMEM((chunks, 2 * fr, wide), bf16),
            pltpu.VMEM((planes, 2 * fr, wide), bf16),
            pltpu.VMEM((2 * fr, wide), bf16),
            pltpu.VMEM((len(OFFSETS), 2 * fr, wide), bf16),
            pltpu.VMEM((chunks, ext, 2 * wide), bf16),
            pltpu.VMEM((ext, cols), f32),
            pltpu.SemaphoreType.DMA((2,)),
            pltpu.SemaphoreType.DMA((2,)),
            pltpu.SemaphoreType.DMA((2,)),
            pltpu.SemaphoreType.DMA((2,)),
            pltpu.SemaphoreType.DMA((chunks,)),
            pltpu.SemaphoreType.DMA((planes,)),
            pltpu.SemaphoreType.DMA((len(OFFSETS),)),
            pltpu.SemaphoreType.DMA((len(OFFSETS),)),
            pltpu.SemaphoreType.DMA((planes,)),
            pltpu.SemaphoreType.DMA((chunks,)),
        ],
        compiler_params=pltpu.CompilerParams(
            collective_id=0, has_side_effects=True, vmem_limit_bytes=48 * 2**20
        ),
        cost_estimate=pl.CostEstimate(
            flops=2 * cols * 2 * fc * (win + ext + 4 * kern * rows),
            bytes_accessed=4 * (3 * rows * cols + 2 * kern * fr * fc),
            transcendentals=0,
        ),
    )(freqs, defocus_ids, phi, target, kernels, psi)


def solution(mesh):
    return jax.shard_map(
        functools.partial(on_device, mesh.shape["strip"], mesh.shape["focus"]),
        mesh=mesh,
        in_specs=(
            P(("tile", "strip"), None),
            P(("tile", "strip"), None),
            P(("tile", "focus")),
            P(),
            P(),
            P(),
            P(),
        ),
        out_specs=P(("tile", "strip"), None),
        check_vma=False,
    )
```

time: 143 us -> 40.6 us (0.28); the launches traced: 141 us -> 40.3 us
  other arithmetic: 49 us -> 0.08 us
  waiting for transfers between devices: 40.8 us -> 0 us
  Pallas kernels: 0 us -> 34 us
  starting transfers between devices: 18.7 us -> 0 us
  matrix products: 17.2 us -> 0 us
  between operations: 14.6 us -> 0.69 us
  local copies, waits for them, and re-layouts: 0.39 us -> 5.58 us
    psum x1 -> x0, waiting for transfers between devices: 37.2 us -> none  [on_device(): lax.psum(y_im.astype(jnp.bfloat16), 'focus').astype(jnp.float32)]
    pallas_call x0 -> x1, Pallas kernels: none -> 34 us  [on_device(): pl.pallas_call(functools.partial(kernel, strips, planes), out_shape=jax.S...]
    convert_element_type x8 -> x1, other arithmetic: 24.5 us -> 0.08 us  [on_device(): jnp.concatenate([col_freqs, row_freqs, row_freqs, filler])]
    ppermute x8 -> x0, starting transfers between devices: 18.7 us -> none  [the longest x4 13.5 us: padded_2(): lax.ppermute(lax.slice_in_dim(block, block.shape[dim] - width, None, axis...]
    dot_general x24 -> x0, matrix products: 17.2 us -> none  [the longest x5 6.07 us: product(): return jnp.dot(lhs_mat, rhs_mat, preferred_element_type=jnp.float32)]
    neg x1 -> x0, other arithmetic: 16.9 us -> none  [on_device(): forward = jnp.concatenate([col_cos, -col_sin], axis=0)]
    unnamed x22 -> x13, local copies, waits for them, and re-layouts: 0.35 us -> 5.5 us
    ppermute x8 -> x0, waiting for transfers between devices: 3.53 us -> none  [the longest x4 3.52 us: padded_2(): lax.ppermute(lax.slice_in_dim(block, 0, width, axis=dim), axis, backward)]
  transfers between devices with their start and end apart: 9 -> 0, of which waited for: 3 -> 0; matrix products, arithmetic and copies ran while one was open for 29% -> 0% of each run, Pallas kernels for 0% -> 0%
where the time goes in v1:
time: 40.6 us; the launch traced here: 40.3 us
  Pallas kernels  34 us (84%)
  local copies, waits for them, and re-layouts  5.58 us (14%)
  between operations  0.69 us (2%)
    pallas_call x1, Pallas kernels, on_device(): pl.pallas_call(functools.partial(kernel, strips, planes), out_shape=jax.S...  34 us
    unnamed x13, local copies, waits for them, and re-layouts  5.5 us

profile of v1, /device:TPU:0, one launch (start us, length us, event | category | flops | bytes accessed | tf_op | source)
XLA Modules:
  0.0 40.3 jit_solution(14689912248326687387)
XLA Ops:
  0.7 0.0 copy-start.4
  0.7 0.0 copy-start.5
  0.7 0.1 pad.3.clone
  0.8 0.6 %copy-done.4 = s32[512]{0:T(512)S(1)} copy-done((s32[512]{0:T(512)S(1)}, s32[512]{0:T(512)}, u32[]{:S(2)}) %copy-start.4) | copy-done | bytes 2072
  1.3 0.0 copy-done.5
  1.4 0.1 fusion.freqs_ref
  1.4 0.0 copy-start
  1.4 1.1 %copy-done = f32[2,4,48,512]{3,2,1,0:T(8,128)S(1)} copy-done((f32[2,4,48,512]{3,2,1,0:T(8,128)S(1)}, f32[2,4,48,512]{3,2,1,0:T(8,128)}, u32[]{:S(2)}) %copy-start) | copy-done | bytes 786456
  2.6 0.0 copy-start.1
  2.6 1.0 %copy-done.1 = f32[64,2048]{1,0:T(8,128)S(1)} copy-done((f32[64,2048]{1,0:T(8,128)S(1)}, f32[64,2048]{1,0:T(8,128)}, u32[]{:S(2)}) %copy-start.1) | copy-done | bytes 524312
  3.6 0.0 copy-start.2
  3.6 1.0 %copy-done.2 = s32[64,2048]{1,0:T(8,128)S(1)} copy-done((s32[64,2048]{1,0:T(8,128)S(1)}, s32[64,2048]{1,0:T(8,128)}, u32[]{:S(2)}) %copy-start.2) | copy-done | bytes 524312
  4.6 0.0 copy-start.3
  4.6 0.9 %copy-done.3 = f32[48,512]{1,0:T(8,128)S(1)} copy-done((f32[48,512]{1,0:T(8,128)S(1)}, f32[48,512]{1,0:T(8,128)}, u32[]{:S(2)}) %copy-start.3) | copy-done | bytes 98328
  5.5 34.0 %shard_map.73 = f32[64,2048]{1,0:T(8,128)S(1)} custom-call(f32[1,640]{1,0:T(1,128)S(1)} %fusion.freqs_ref, s32[1]{0:T(128)S(6)} %copy.9.defocus_ref, f32[64,2048]{1,0:T(8,128)S(1)} %copy-done.1, s32[64,2048]{1,0:T(8,128)S(1)} %copy-done.2, f32[2,4,48,512]{3,2,1,0:T(8,128)S(1)} %copy-done, f32[48,512]{1,0:T(8,128)S(1)} %copy-done.3), custom_call_target="tpu_custom_call" | custom-call | flops 5435817984 | bytes 2359296 | tf_op jit(solution)/shard_map/pallas_call | solution.py:510
  39.5 0.8 %copy.10 = f32[64,2048]{1,0:T(8,128)} copy(f32[64,2048]{1,0:T(8,128)S(1)} %shard_map.73) | data formatting | bytes 1048576
  (1 shorter events, 0.0 us)
Async XLA Ops:
  0.7 0.7 %copy-start.4 = (s32[512]{0:T(512)S(1)}, s32[512]{0:T(512)}, u32[]{:S(2)}) copy-start(s32[512]{0:T(512)} %param.13) | copy-start | bytes 6148
  0.7 0.7 %copy-start.5 = (s32[48]{0:T(128)S(1)}, s32[48]{0:T(128)}, u32[]{:S(2)}) copy-start(s32[48]{0:T(128)} %param.12) | copy-start | bytes 580
  1.4 1.1 %copy-start = (f32[2,4,48,512]{3,2,1,0:T(8,128)S(1)}, f32[2,4,48,512]{3,2,1,0:T(8,128)}, u32[]{:S(2)}) copy-start(f32[2,4,48,512]{3,2,1,0:T(8,128)} %kernels_ref.1) | copy-start | bytes 2359300
  2.6 1.0 %copy-start.1 = (f32[64,2048]{1,0:T(8,128)S(1)}, f32[64,2048]{1,0:T(8,128)}, u32[]{:S(2)}) copy-start(f32[64,2048]{1,0:T(8,128)} %phi_ref.1) | copy-start | bytes 1572868
  3.6 1.0 %copy-start.2 = (s32[64,2048]{1,0:T(8,128)S(1)}, s32[64,2048]{1,0:T(8,128)}, u32[]{:S(2)}) copy-start(s32[64,2048]{1,0:T(8,128)} %target_ref.1) | copy-start | bytes 1572868
  4.6 0.9 %copy-start.3 = (f32[48,512]{1,0:T(8,128)S(1)}, f32[48,512]{1,0:T(8,128)}, u32[]{:S(2)}) copy-start(f32[48,512]{1,0:T(8,128)} %psi_ref.1) | copy-start | bytes 294916

commit v2 on v1

--- a/solution.py
+++ b/solution.py
@@ -54,12 +54,6 @@
     return jnp.dot(lhs, rhs, preferred_element_type=jnp.float32)
 
 
-def dot_t(lhs, rhs):
-    return lax.dot_general(
-        lhs, rhs, (((1,), (1,)), ((), ())), preferred_element_type=jnp.float32
-    )
-
-
 def iota(shape, dim):
     return lax.broadcasted_iota(jnp.int32, shape, dim)
 
@@ -67,14 +61,23 @@
 def kernel(
     strips,
     planes,
-    freqs_ref,
     defocus_ref,
+    phi_hbm,
+    target_hbm,
+    kernels_hbm,
+    psi_hbm,
+    row_freqs_hbm,
+    col_freqs_hbm,
+    out_ref,
     phi_ref,
     target_ref,
     kernels_ref,
     psi_ref,
-    out_ref,
+    row_freqs_ref,
+    col_freqs_ref,
+    load_sem,
     table,
+    table_t,
     freq_col,
     window,
     halo,
@@ -91,6 +94,8 @@
     y_side,
     z_ref,
     grad,
+    slope_ref,
+    level_ref,
     mask_send,
     mask_recv,
     halo_send,
@@ -138,6 +143,22 @@
             device_id_type=MESH,
         )
 
+    pairs = (
+        (phi_hbm, phi_ref),
+        (col_freqs_hbm, col_freqs_ref),
+        (row_freqs_hbm, row_freqs_ref),
+        (psi_hbm, psi_ref),
+        (kernels_hbm, kernels_ref),
+        (target_hbm, target_ref),
+    )
+    loads = [
+        pltpu.make_async_copy(src, dst, load_sem.at[index])
+        for index, (src, dst) in enumerate(pairs)
+    ]
+    for load in loads:
+        load.start()
+    phi_load, col_load, row_load, psi_load, kernels_load, target_load = loads
+
     barrier = pltpu.get_barrier_semaphore()
     for offset in OFFSETS:
 
@@ -155,42 +176,20 @@
             device_id_type=MESH,
         )
 
+    phi_load.wait()
     window[MARGIN : MARGIN + rows, :] = jnp.tanh(phi_ref[...]).astype(bf16)
 
-    beside = jnp.minimum(strip, 2) + jnp.minimum(strips - 1 - strip, 2)
-    pl.semaphore_wait(barrier, planes - 1 + beside)
-
-    def mask_copy(offset):
-        if offset == 1:
-            src, dst, slot = window.at[rows : rows + MARGIN], window.at[:MARGIN], 0
-        else:
-            src, dst, slot = window.at[MARGIN : 2 * MARGIN], window.at[MARGIN + rows :], 1
-        return to_strip(src, dst, mask_send.at[slot], mask_recv.at[slot], offset)
-
-    def halo_copy(offset):
-        if offset == 1:
-            src, slot = phi_ref.at[rows - HALO :], 0
-        else:
-            src, slot = phi_ref.at[:HALO], 1
-        return to_strip(src, halo.at[slot], halo_send.at[slot], halo_recv.at[slot], offset)
-
-    for copy in (mask_copy, halo_copy):
-        for offset in (1, -1):
-
-            @pl.when(inside(offset))
-            def _(copy=copy, offset=offset):
-                copy(offset).start()
-
+    col_load.wait()
+    col_lane = col_freqs_ref[...].astype(jnp.float32)
     for block in range(fc // LANES):
-        lane_freqs = freqs_ref[:, block * LANES : (block + 1) * LANES]
         freq_col[block * LANES : (block + 1) * LANES, :] = jnp.broadcast_to(
-            lane_freqs, (LANES, LANES)
+            col_lane[:, block * LANES : (block + 1) * LANES], (LANES, LANES)
         ).T
     group = 32
-    for chunk in range(chunks):
-
+
+    def table_rows(chunk):
         @pl.loop(0, wide // group)
-        def _(step, chunk=chunk):
+        def _(step):
             first = pl.multiple_of(step * group, group)
             freq = freq_col[pl.ds(chunk * wide + first, group), :]
             lane = iota((group, LANES), 1).astype(jnp.float32)
@@ -205,7 +204,61 @@
                     sin_now * cos_turn + cos_now * sin_turn,
                 )
 
-    row_lane = freqs_ref[:, fc : fc + LANES]
+    segment = 16 * group
+
+    def table_columns(block):
+        freq = jnp.broadcast_to(col_lane[:, block * LANES : (block + 1) * LANES], (group, LANES))
+        cos_turn, sin_turn = turn_pair(whole_turns(freq * float(group), float(cols)))
+        at_cos = 2 * (block * LANES // wide) * wide + block * LANES % wide
+
+        @pl.loop(0, cols // segment)
+        def _(step):
+            first = pl.multiple_of(step * segment, segment)
+            place = (first + iota((group, LANES), 0)).astype(jnp.float32)
+            cos_now, sin_now = turn_pair(whole_turns(freq * place, float(cols)))
+            for part in range(segment // group):
+                here = pl.ds(first + part * group, group)
+                table_t[here, at_cos : at_cos + LANES] = cos_now.astype(bf16)
+                table_t[here, at_cos + wide : at_cos + wide + LANES] = sin_now.astype(bf16)
+                cos_now, sin_now = (
+                    cos_now * cos_turn - sin_now * sin_turn,
+                    sin_now * cos_turn + cos_now * sin_turn,
+                )
+
+    for block in range(fc // LANES):
+        table_columns(block)
+
+    beside = jnp.minimum(strip, 2) + jnp.minimum(strips - 1 - strip, 2)
+    pl.semaphore_wait(barrier, planes - 1 + beside)
+
+    def mask_copy(offset):
+        if offset == 1:
+            src, dst, slot = window.at[rows : rows + MARGIN], window.at[:MARGIN], 0
+        else:
+            src, dst, slot = window.at[MARGIN : 2 * MARGIN], window.at[MARGIN + rows :], 1
+        return to_strip(src, dst, mask_send.at[slot], mask_recv.at[slot], offset)
+
+    def halo_copy(offset):
+        if offset == 1:
+            src, slot = phi_ref.at[rows - HALO :], 0
+        else:
+            src, slot = phi_ref.at[:HALO], 1
+        return to_strip(src, halo.at[slot], halo_send.at[slot], halo_recv.at[slot], offset)
+
+    for offset in (1, -1):
+
+        @pl.when(inside(offset))
+        def _(offset=offset):
+            mask_copy(offset).start()
+
+    for chunk in range(chunks):
+        table_rows(chunk)
+
+    row_load.wait()
+    row_once = row_freqs_ref[...].astype(jnp.float32)
+    row_lane = jnp.concatenate(
+        [row_once, row_once, jnp.zeros((1, LANES - both), jnp.float32)], axis=1
+    )
     row_sub = jnp.broadcast_to(row_lane, (LANES, LANES)).T[:both, :1]
     row_lane = row_lane[:, :both]
 
@@ -232,6 +285,8 @@
 
     middle = (LEVELS - 1) / 2.0
     defocus = (defocus_ref[0].astype(jnp.float32) - middle) * (1.0 / middle)
+    psi_load.wait()
+    kernels_load.wait()
     cos_turn, sin_turn = turn_pair(psi_ref[...] * (defocus * (0.5 / jnp.pi)))
     for k in range(kern):
         best_re, best_im = kernels_ref[0, k], kernels_ref[1, k]
@@ -254,7 +309,13 @@
     @pl.loop(0, chunks)
     def _(chunk):
         here = pl.ds(pl.multiple_of(chunk * 2 * wide, 2 * wide), 2 * wide)
-        spec[:, here] = dot_t(window[...], table[here, :]).astype(bf16)
+        spec[:, here] = dot(window[...], table_t[:, here]).astype(bf16)
+
+    for offset in (1, -1):
+
+        @pl.when(inside(offset))
+        def _(offset=offset):
+            halo_copy(offset).start()
 
     halves = dot(row_all, spec[...])
     for k in range(kern):
@@ -283,11 +344,17 @@
             q_ref[turned, at_sin] = q_re
 
     piece = 256
-
-    @pl.loop(0, cols // piece)
-    def _(step):
-        here = pl.ds(pl.multiple_of(step * piece, piece), piece)
-        field = dot(q_ref[...], table[:, here]).reshape(2 * kern, rows, piece)
+    target_load.wait()
+
+    def fields(step):
+        return dot(q_ref[...], table[:, step * piece : (step + 1) * piece])
+
+    ahead = fields(0)
+    for step in range(cols // piece):
+        here = slice(step * piece, (step + 1) * piece)
+        field = ahead.reshape(2 * kern, rows, piece)
+        if (step + 1) * piece < cols:
+            ahead = fields(step + 1)
         intensity = (norm * norm / kern) * jnp.sum(field * field, axis=0)
         resist = 1.0 / (1.0 + jnp.exp(-slope_resist * (intensity - level_resist)))
         weight = (
@@ -302,7 +369,7 @@
 
     def adjoint(chunk):
         here = pl.ds(pl.multiple_of(chunk * 2 * wide, 2 * wide), 2 * wide)
-        u_all = dot_t(v_ref[...], table[here, :])
+        u_all = dot(v_ref[...], table_t[:, here])
         u_re = (u_all[:half, :wide] + u_all[half:, wide:]).astype(bf16)
         u_im = (u_all[half:, :wide] - u_all[:half, wide:]).astype(bf16)
         stacked = jnp.concatenate(
@@ -357,6 +424,29 @@
         covered = jnp.logical_and(place >= 0, place < win)
         row_out[index] = jnp.where(covered, values, 0.0).astype(bf16)
 
+    for index, offset in enumerate((-1, 1)):
+
+        @pl.when(inside(offset))
+        def _(offset=offset):
+            halo_copy(-offset).wait_recv()
+
+        @pl.when(jnp.logical_not(inside(offset)))
+        def _(index=index):
+            halo[index] = jnp.zeros((HALO, cols), jnp.float32)
+
+    row_place = strip * rows + iota((ext, LANES), 0) - HALO
+    kept = jnp.where(
+        jnp.logical_and(row_place >= 0, row_place < strips * rows), 1.0, 0.0
+    ).astype(jnp.float32)
+    for spot, values in (
+        (slice(0, HALO), halo.at[0]),
+        (slice(HALO, HALO + rows), phi_ref),
+        (slice(HALO + rows, ext), halo.at[1]),
+    ):
+        level_ref[0, spot, :] = values[...]
+        mask = jnp.tanh(values[...])
+        slope_ref[spot, :] = (step_size * norm) * (1.0 - mask * mask) * kept[spot, :1]
+
     def side_copy(offset):
         slot = OFFSETS.index(-offset)
         return to_strip(y_sum, y_side.at[slot], side_send.at[slot], side_recv.at[slot], offset)
@@ -401,66 +491,66 @@
     else:
         own_part()
 
-    def part_grad(chunk):
-        here = pl.ds(pl.multiple_of(chunk * 2 * wide, 2 * wide), 2 * wide)
-        return dot(z_ref[chunk], table[here, :])
+    def arrived(chunk):
+        to_focus(
+            z_ref.at[chunk], z_ref.at[chunk], ag_send.at[0], ag_recv.at[chunk], chunk * stride
+        ).wait_recv()
 
     for step in range(chunks):
         chunk = lax.rem(mine + step, chunks)
         if step:
-            to_focus(
-                z_ref.at[chunk], z_ref.at[chunk], ag_send.at[0], ag_recv.at[chunk], chunk * stride
-            ).wait_recv()
-            grad[...] += part_grad(chunk)
-        else:
-            if stride > 1:
-
-                @pl.when(jnp.logical_not(owner))
-                def _(chunk=chunk):
-                    to_focus(
-                        z_ref.at[chunk],
-                        z_ref.at[chunk],
-                        ag_send.at[0],
-                        ag_recv.at[chunk],
-                        chunk * stride,
-                    ).wait_recv()
-
-            grad[...] = part_grad(chunk)
-
-    for index, offset in enumerate((-1, 1)):
-
-        @pl.when(inside(offset))
-        def _(offset=offset):
-            halo_copy(-offset).wait_recv()
-
-        @pl.when(jnp.logical_not(inside(offset)))
-        def _(index=index):
-            halo[index] = jnp.zeros((HALO, cols), jnp.float32)
-
-    level = jnp.concatenate([halo[0], phi_ref[...], halo[1]], axis=0)
-    slope = jnp.tanh(level)
-    row_place = strip * rows + iota((ext, cols), 0) - HALO
-    in_tile = jnp.logical_and(row_place >= 0, row_place < strips * rows)
-    level = level - (step_size * norm) * (1.0 - slope * slope) * grad[...]
-    level = jnp.where(in_tile, level, 0.0)
-    column = iota((ext, cols), 1)
+            arrived(chunk)
+        elif stride > 1:
+
+            @pl.when(jnp.logical_not(owner))
+            def _(chunk=chunk):
+                arrived(chunk)
+
+        here = pl.ds(pl.multiple_of(chunk * 2 * wide, 2 * wide), 2 * wide)
+        for start in range(0, cols, piece):
+            there = slice(start, start + piece)
+            part = dot(z_ref[chunk], table[here, there])
+            if step:
+                part += grad[:, there]
+            if step < chunks - 1:
+                grad[:, there] = part
+            else:
+                level_ref[0, :, there] = level_ref[0, :, there] - slope_ref[:, there] * part
+
+    lane = iota((ext, LANES), 1)
+    empty = jnp.zeros((ext, LANES), jnp.float32)
+    blocks = cols // LANES
     for sweep in range(SWEEPS):
-        right = jnp.where(column == cols - 1, 0.0, pltpu.roll(level, cols - 1, 1))
-        left = jnp.where(column == 0, 0.0, pltpu.roll(level, 1, 1))
-        across = right - left
-        upper = pltpu.roll(level, ext - 1, 0)
-        lower = pltpu.roll(level, 1, 0)
-        diagonal = pltpu.roll(across, ext - 1, 0) - pltpu.roll(across, 1, 0)
-        grad_x = 0.5 * (upper - lower)
-        grad_y = 0.5 * across
-        second_x = upper - 2.0 * level + lower
-        second_y = right - 2.0 * level + left
-        cross = 0.25 * diagonal
-        flow = (
-            second_x * grad_y * grad_y - 2.0 * grad_x * grad_y * cross + second_y * grad_x * grad_x
-        ) / (1.0 + grad_x * grad_x + grad_y * grad_y)
-        level = jnp.where(in_tile, level + flow_rate * flow, 0.0)
-    out_ref[...] = level[HALO : HALO + rows]
+
+        def load(block, sweep=sweep):
+            if not 0 <= block < blocks:
+                return empty, empty, empty
+            center = level_ref[sweep % 2, :, block * LANES : (block + 1) * LANES]
+            return center, pltpu.roll(center, LANES - 1, 1), pltpu.roll(center, 1, 1)
+
+        before, now, after = load(-1), load(0), load(1)
+        for block in range(blocks):
+            level = now[0]
+            right = jnp.where(lane == LANES - 1, after[1], now[1])
+            left = jnp.where(lane == 0, before[2], now[2])
+            across = right - left
+            upper = pltpu.roll(level, ext - 1, 0)
+            lower = pltpu.roll(level, 1, 0)
+            along = upper - lower
+            diagonal = pltpu.roll(across, ext - 1, 0) - pltpu.roll(across, 1, 0)
+            twice = 2.0 * level
+            second_x = upper + lower - twice
+            second_y = right + left - twice
+            along_2 = along * along
+            across_2 = across * across
+            flow = second_x * across_2 - 0.5 * (along * across) * diagonal + second_y * along_2
+            level = level + flow_rate * flow / (4.0 + along_2 + across_2)
+            there = slice(block * LANES, (block + 1) * LANES)
+            if sweep < SWEEPS - 1:
+                level_ref[(sweep + 1) % 2, :, there] = level * kept
+            else:
+                out_ref[:, there] = level[HALO : HALO + rows]
+            before, now, after = now, after, load(block + 2)
 
     for copy in (mask_copy, halo_copy):
         for offset in (1, -1):
@@ -502,18 +592,25 @@
     chunks = fc // wide
     ext = rows + 2 * HALO
     win = rows + 2 * MARGIN
-    filler = jnp.zeros((LANES - 2 * fr,), jnp.int32)
-    freqs = jnp.concatenate([col_freqs, row_freqs, row_freqs, filler]).astype(jnp.float32)[None]
     vmem = pl.BlockSpec(memory_space=pltpu.VMEM)
+    anywhere = pl.BlockSpec(memory_space=pl.ANY)
     smem = pl.BlockSpec(memory_space=pltpu.SMEM)
     bf16, f32 = jnp.bfloat16, jnp.float32
     return pl.pallas_call(
         functools.partial(kernel, strips, planes),
         out_shape=jax.ShapeDtypeStruct((rows, cols), f32),
-        in_specs=[vmem, smem, vmem, vmem, vmem, vmem],
+        in_specs=[smem] + [anywhere] * 6,
         out_specs=vmem,
         scratch_shapes=[
+            pltpu.VMEM(phi.shape, phi.dtype),
+            pltpu.VMEM(target.shape, target.dtype),
+            pltpu.VMEM(kernels.shape, kernels.dtype),
+            pltpu.VMEM(psi.shape, psi.dtype),
+            pltpu.VMEM((1, fr), row_freqs.dtype),
+            pltpu.VMEM((1, fc), col_freqs.dtype),
+            pltpu.SemaphoreType.DMA((6,)),
             pltpu.VMEM((2 * fc, cols), bf16),
+            pltpu.VMEM((cols, 2 * fc), bf16),
             pltpu.VMEM((fc, LANES), f32),
             pltpu.VMEM((win, cols), bf16),
             pltpu.VMEM((2, HALO, cols), f32),
@@ -530,6 +627,8 @@
             pltpu.VMEM((len(OFFSETS), 2 * fr, wide), bf16),
             pltpu.VMEM((chunks, ext, 2 * wide), bf16),
             pltpu.VMEM((ext, cols), f32),
+            pltpu.VMEM((ext, cols), f32),
+            pltpu.VMEM((2, ext, cols), f32),
             pltpu.SemaphoreType.DMA((2,)),
             pltpu.SemaphoreType.DMA((2,)),
             pltpu.SemaphoreType.DMA((2,)),
@@ -542,14 +641,14 @@
             pltpu.SemaphoreType.DMA((chunks,)),
         ],
         compiler_params=pltpu.CompilerParams(
-            collective_id=0, has_side_effects=True, vmem_limit_bytes=48 * 2**20
+            collective_id=0, has_side_effects=True, vmem_limit_bytes=56 * 2**20
         ),
         cost_estimate=pl.CostEstimate(
             flops=2 * cols * 2 * fc * (win + ext + 4 * kern * rows),
             bytes_accessed=4 * (3 * rows * cols + 2 * kern * fr * fc),
             transcendentals=0,
         ),
-    )(freqs, defocus_ids, phi, target, kernels, psi)
+    )(defocus_ids, phi, target, kernels, psi, row_freqs[None], col_freqs[None])
 
 
 def solution(mesh):

time: 40.6 us -> 36.2 us (0.89)
  local copies, waits for them, and re-layouts: 5.58 us -> 1.87 us
  Pallas kernels: 34 us -> 33.4 us
    unnamed x13 -> x1, local copies, waits for them, and re-layouts: 5.5 us -> 1.87 us
    pallas_call x1, Pallas kernels: 34 us -> 33.4 us  [on_device(): pl.pallas_call(functools.partial(kernel, strips, planes), out_shape=jax.S...]
where the time goes in v2:
time: 36.2 us; the launch traced here: 36 us
  Pallas kernels  33.4 us (92%)
  local copies, waits for them, and re-layouts  1.87 us (5%)
  between operations  0.66 us (2%)
    pallas_call x1, Pallas kernels, on_device(): pl.pallas_call(functools.partial(kernel, strips, planes), out_shape=jax.S...  33.4 us
    unnamed x1, local copies, waits for them, and re-layouts  1.87 us

profile of v2, /device:TPU:0, one launch (start us, length us, event | category | flops | bytes accessed | tf_op | source)
XLA Modules:
  0.0 36.0 jit_solution(13987221059086851272)
XLA Ops:
  0.7 33.4 %shard_map.73 = f32[64,2048]{1,0:T(8,128)} custom-call(s32[1]{0:T(128)S(6)} %copy.9.defocus_ref, f32[64,2048]{1,0:T(8,128)} %phi_hbm.1, s32[64,2048]{1,0:T(8,128)} %target_hbm.1, f32[2,4,48,512]{3,2,1,0:T(8,128)} %kernels_hbm.1, f32[48,512]{1,0:T(8,128)} %psi_hbm.1, s32[1,48]{1,0:T(1,128)} %bitcast.3, s32[1,512]{1,0:T(1,128)} %bitcast.2), custom_call_target="tpu_custom_call" | custom-call | flops 5435817984 | bytes 2359296 | tf_op jit(solution)/shard_map/pallas_call | solution.py:599
  34.1 1.9 %copy.10 = f32[64,2048]{1,0:T(8,128)} copy(f32[64,2048]{1,0:T(8,128)} %shard_map.73) | data formatting | bytes 1048576

commit v3 on v2

--- a/solution.py
+++ b/solution.py
@@ -68,7 +68,8 @@
     psi_hbm,
     row_freqs_hbm,
     col_freqs_hbm,
-    out_ref,
+    base_hbm,
+    flow_hbm,
     phi_ref,
     target_ref,
     kernels_ref,
@@ -96,6 +97,8 @@
     grad,
     slope_ref,
     level_ref,
+    flow_ref,
+    store_sem,
     mask_send,
     mask_recv,
     halo_send,
@@ -144,8 +147,8 @@
         )
 
     pairs = (
+        (col_freqs_hbm, col_freqs_ref),
         (phi_hbm, phi_ref),
-        (col_freqs_hbm, col_freqs_ref),
         (row_freqs_hbm, row_freqs_ref),
         (psi_hbm, psi_ref),
         (kernels_hbm, kernels_ref),
@@ -157,7 +160,7 @@
     ]
     for load in loads:
         load.start()
-    phi_load, col_load, row_load, psi_load, kernels_load, target_load = loads
+    col_load, phi_load, row_load, psi_load, kernels_load, target_load = loads
 
     barrier = pltpu.get_barrier_semaphore()
     for offset in OFFSETS:
@@ -176,8 +179,6 @@
             device_id_type=MESH,
         )
 
-    phi_load.wait()
-    window[MARGIN : MARGIN + rows, :] = jnp.tanh(phi_ref[...]).astype(bf16)
 
     col_load.wait()
     col_lane = col_freqs_ref[...].astype(jnp.float32)
@@ -225,18 +226,18 @@
                     sin_now * cos_turn + cos_now * sin_turn,
                 )
 
-    for block in range(fc // LANES):
-        table_columns(block)
-
-    beside = jnp.minimum(strip, 2) + jnp.minimum(strips - 1 - strip, 2)
-    pl.semaphore_wait(barrier, planes - 1 + beside)
-
-    def mask_copy(offset):
+    def spec_copy(offset, chunk):
         if offset == 1:
-            src, dst, slot = window.at[rows : rows + MARGIN], window.at[:MARGIN], 0
+            src, dst, slot = slice(rows, rows + MARGIN), slice(0, MARGIN), 0
         else:
-            src, dst, slot = window.at[MARGIN : 2 * MARGIN], window.at[MARGIN + rows :], 1
-        return to_strip(src, dst, mask_send.at[slot], mask_recv.at[slot], offset)
+            src, dst, slot = slice(MARGIN, 2 * MARGIN), slice(MARGIN + rows, win), 1
+        return to_strip(
+            spec.at[chunk, src],
+            spec.at[chunk, dst],
+            mask_send.at[slot, chunk],
+            mask_recv.at[slot, chunk],
+            offset,
+        )
 
     def halo_copy(offset):
         if offset == 1:
@@ -245,12 +246,30 @@
             src, slot = phi_ref.at[:HALO], 1
         return to_strip(src, halo.at[slot], halo_send.at[slot], halo_recv.at[slot], offset)
 
-    for offset in (1, -1):
-
-        @pl.when(inside(offset))
-        def _(offset=offset):
-            mask_copy(offset).start()
-
+    def send_spec(chunk):
+        for offset in (1, -1):
+
+            @pl.when(inside(offset))
+            def _(offset=offset):
+                spec_copy(offset, chunk).start()
+
+    greet = min(1, chunks - 1)
+    for chunk in range(chunks):
+        for block in range(chunk * wide // LANES, (chunk + 1) * wide // LANES):
+            table_columns(block)
+        if chunk == 0:
+            phi_load.wait()
+            window[...] = jnp.tanh(phi_ref[...]).astype(bf16)
+        spec[chunk, MARGIN : MARGIN + rows, :] = dot(
+            window[...], table_t[:, 2 * chunk * wide : 2 * (chunk + 1) * wide]
+        ).astype(bf16)
+        if chunk == greet:
+            beside = jnp.minimum(strip, 2) + jnp.minimum(strips - 1 - strip, 2)
+            pl.semaphore_wait(barrier, planes - 1 + beside)
+            for earlier in range(chunk):
+                send_spec(earlier)
+        if chunk >= greet:
+            send_spec(chunk)
     for chunk in range(chunks):
         table_rows(chunk)
 
@@ -296,20 +315,19 @@
             k_re[k, chunk] = full_re[:, chunk * wide : (chunk + 1) * wide]
             k_im[k, chunk] = full_im[:, chunk * wide : (chunk + 1) * wide]
 
-    for offset, copy, spot in ((-1, 1, slice(0, MARGIN)), (1, -1, slice(MARGIN + rows, win))):
-
-        @pl.when(inside(offset))
-        def _(copy=copy):
-            mask_copy(copy).wait_recv()
-
-        @pl.when(jnp.logical_not(inside(offset)))
-        def _(spot=spot):
-            window[spot, :] = jnp.zeros((MARGIN, cols), bf16)
-
-    @pl.loop(0, chunks)
-    def _(chunk):
-        here = pl.ds(pl.multiple_of(chunk * 2 * wide, 2 * wide), 2 * wide)
-        spec[:, here] = dot(window[...], table_t[:, here]).astype(bf16)
+    halves = []
+    for chunk in range(chunks):
+        for offset, spot in ((-1, slice(0, MARGIN)), (1, slice(MARGIN + rows, win))):
+
+            @pl.when(inside(offset))
+            def _(offset=offset, chunk=chunk):
+                spec_copy(-offset, chunk).wait_recv()
+
+            @pl.when(jnp.logical_not(inside(offset)))
+            def _(spot=spot, chunk=chunk):
+                spec[chunk, spot, :] = jnp.zeros((MARGIN, 2 * wide), bf16)
+
+        halves.append(dot(row_all, spec[chunk]))
 
     for offset in (1, -1):
 
@@ -317,14 +335,12 @@
         def _(offset=offset):
             halo_copy(offset).start()
 
-    halves = dot(row_all, spec[...])
     for k in range(kern):
         tops, lows = [], []
         for chunk in range(chunks):
-            at_cos = slice(2 * chunk * wide, (2 * chunk + 1) * wide)
-            at_sin = slice((2 * chunk + 1) * wide, (2 * chunk + 2) * wide)
-            s_re = norm * (halves[:fr, at_cos] - halves[fr:, at_sin])
-            s_im = -norm * (halves[:fr, at_sin] + halves[fr:, at_cos])
+            rows_cos, rows_sin = halves[chunk][:fr], halves[chunk][fr:]
+            s_re = norm * (rows_cos[:, :wide] - rows_sin[:, wide:])
+            s_im = -norm * (rows_cos[:, wide:] + rows_sin[:, :wide])
             tops.append(k_re[k, chunk] * s_re - k_im[k, chunk] * s_im)
             lows.append(k_re[k, chunk] * s_im + k_im[k, chunk] * s_re)
         g_pair = jnp.concatenate(
@@ -520,7 +536,21 @@
     lane = iota((ext, LANES), 1)
     empty = jnp.zeros((ext, LANES), jnp.float32)
     blocks = cols // LANES
+    span = max(1, blocks // 4)
+    last = (SWEEPS - 1) % 2
+
+    def store(part):
+        here = slice(part * span * LANES, (part + 1) * span * LANES)
+        return pltpu.make_async_copy(
+            flow_ref.at[:, here], flow_hbm.at[:, here], store_sem.at[1 + part]
+        )
+
+    store_base = pltpu.make_async_copy(
+        level_ref.at[last, HALO : HALO + rows], base_hbm, store_sem.at[0]
+    )
     for sweep in range(SWEEPS):
+        if sweep == SWEEPS - 1:
+            store_base.start()
 
         def load(block, sweep=sweep):
             if not 0 <= block < blocks:
@@ -544,20 +574,27 @@
             along_2 = along * along
             across_2 = across * across
             flow = second_x * across_2 - 0.5 * (along * across) * diagonal + second_y * along_2
-            level = level + flow_rate * flow / (4.0 + along_2 + across_2)
+            flow = flow_rate * flow / (4.0 + along_2 + across_2)
             there = slice(block * LANES, (block + 1) * LANES)
             if sweep < SWEEPS - 1:
-                level_ref[(sweep + 1) % 2, :, there] = level * kept
+                level_ref[(sweep + 1) % 2, :, there] = (level + flow) * kept
             else:
-                out_ref[:, there] = level[HALO : HALO + rows]
+                flow_ref[:, there] = flow[HALO : HALO + rows]
+                if (block + 1) % span == 0:
+                    store(block // span).start()
             before, now, after = now, after, load(block + 2)
 
-    for copy in (mask_copy, halo_copy):
-        for offset in (1, -1):
-
-            @pl.when(inside(offset))
-            def _(copy=copy, offset=offset):
-                copy(offset).wait_send()
+    store_base.wait()
+    for part in range(blocks // span):
+        store(part).wait()
+
+    for offset in (1, -1):
+
+        @pl.when(inside(offset))
+        def _(offset=offset):
+            halo_copy(offset).wait_send()
+            for chunk in range(chunks):
+                spec_copy(offset, chunk).wait_send()
 
     for step in range(chunks):
         chunk = lax.rem(mine + step, chunks)
@@ -592,15 +629,14 @@
     chunks = fc // wide
     ext = rows + 2 * HALO
     win = rows + 2 * MARGIN
-    vmem = pl.BlockSpec(memory_space=pltpu.VMEM)
-    anywhere = pl.BlockSpec(memory_space=pl.ANY)
+    hbm = pl.BlockSpec(memory_space=pltpu.HBM)
     smem = pl.BlockSpec(memory_space=pltpu.SMEM)
     bf16, f32 = jnp.bfloat16, jnp.float32
-    return pl.pallas_call(
+    base, flow = pl.pallas_call(
         functools.partial(kernel, strips, planes),
-        out_shape=jax.ShapeDtypeStruct((rows, cols), f32),
-        in_specs=[smem] + [anywhere] * 6,
-        out_specs=vmem,
+        out_shape=[jax.ShapeDtypeStruct((rows, cols), f32)] * 2,
+        in_specs=[smem] + [hbm] * 6,
+        out_specs=[hbm, hbm],
         scratch_shapes=[
             pltpu.VMEM(phi.shape, phi.dtype),
             pltpu.VMEM(target.shape, target.dtype),
@@ -612,11 +648,11 @@
             pltpu.VMEM((2 * fc, cols), bf16),
             pltpu.VMEM((cols, 2 * fc), bf16),
             pltpu.VMEM((fc, LANES), f32),
-            pltpu.VMEM((win, cols), bf16),
+            pltpu.VMEM((rows, cols), bf16),
             pltpu.VMEM((2, HALO, cols), f32),
             pltpu.VMEM((kern, chunks, fr, wide), f32),
             pltpu.VMEM((kern, chunks, fr, wide), f32),
-            pltpu.VMEM((win, 2 * fc), bf16),
+            pltpu.VMEM((chunks, win, 2 * wide), bf16),
             pltpu.VMEM((2 * kern * rows, 2 * fc), bf16),
             pltpu.VMEM((2 * kern * rows, cols), bf16),
             pltpu.VMEM((1 + len(OFFSETS), 2 * ext, 2 * fr), bf16),
@@ -629,8 +665,10 @@
             pltpu.VMEM((ext, cols), f32),
             pltpu.VMEM((ext, cols), f32),
             pltpu.VMEM((2, ext, cols), f32),
-            pltpu.SemaphoreType.DMA((2,)),
-            pltpu.SemaphoreType.DMA((2,)),
+            pltpu.VMEM((rows, cols), f32),
+            pltpu.SemaphoreType.DMA((1 + cols // LANES,)),
+            pltpu.SemaphoreType.DMA((2, chunks)),
+            pltpu.SemaphoreType.DMA((2, chunks)),
             pltpu.SemaphoreType.DMA((2,)),
             pltpu.SemaphoreType.DMA((2,)),
             pltpu.SemaphoreType.DMA((chunks,)),
@@ -641,7 +679,7 @@
             pltpu.SemaphoreType.DMA((chunks,)),
         ],
         compiler_params=pltpu.CompilerParams(
-            collective_id=0, has_side_effects=True, vmem_limit_bytes=56 * 2**20
+            collective_id=0, has_side_effects=True, vmem_limit_bytes=58 * 2**20
         ),
         cost_estimate=pl.CostEstimate(
             flops=2 * cols * 2 * fc * (win + ext + 4 * kern * rows),
@@ -649,6 +687,7 @@
             transcendentals=0,
         ),
     )(defocus_ids, phi, target, kernels, psi, row_freqs[None], col_freqs[None])
+    return base + flow
 
 
 def solution(mesh):

time: 36.2 us -> 35.5 us (0.981)
  other arithmetic: 0 us -> 2.05 us
  local copies, waits for them, and re-layouts: 1.87 us -> 0 us
  Pallas kernels: 33.4 us -> 32.7 us
    add x0 -> x1, other arithmetic: none -> 2.05 us  [on_device(): return base + flow]
    unnamed x1 -> x0, local copies, waits for them, and re-layouts: 1.87 us -> none
    pallas_call x1, Pallas kernels: 33.4 us -> 32.7 us  [on_device(): pl.pallas_call(functools.partial(kernel, strips, planes), out_shape=[jax....]
where the time goes in v3:
time: 35.5 us; the launch traced here: 35.4 us
  Pallas kernels  32.7 us (92%)
  other arithmetic  2.05 us (6%)
  between operations  0.66 us (2%)
    pallas_call x1, Pallas kernels, on_device(): pl.pallas_call(functools.partial(kernel, strips, planes), out_shape=[jax....  32.7 us
    add x1, other arithmetic, on_device(): return base + flow  2.05 us

profile of v3, /device:TPU:0, one launch (start us, length us, event | category | flops | bytes accessed | tf_op | source)
XLA Modules:
  0.0 35.4 jit_solution(16740871658726117379)
XLA Ops:
  0.7 32.7 %shard_map.73 = (f32[64,2048]{1,0:T(8,128)}, f32[64,2048]{1,0:T(8,128)}) custom-call(s32[1]{0:T(128)S(6)} %copy.8.defocus_ref, f32[64,2048]{1,0:T(8,128)} %phi_hbm.1, s32[64,2048]{1,0:T(8,128)} %target_hbm.1, f32[2,4,48,512]{3,2,1,0:T(8,128)} %kernels_hbm.1, f32[48,512]{1,0:T(8,128)} %psi_hbm.1, s32[1,48]{1,0:T(1,128)} %bitcast.3, s32[1,512]{1,0:T(1,128)} %bitcast.2), custom_call_target="tpu_custom_call" | custom-call | flops 5435817984 | bytes 2359296 | tf_op jit(solution)/shard_map/pallas_call | solution.py:635
  33.3 2.0 %add.3 = f32[64,2048]{1,0:T(8,128)} add(f32[64,2048]{1,0:T(8,128)} %get-tuple-element.7, f32[64,2048]{1,0:T(8,128)} %get-tuple-element.8) | non-fusion elementwise | flops 131072 | bytes 1572864 | tf_op jit(solution)/shard_map/add | solution.py:690

commit v4 on v3

--- a/solution.py
+++ b/solution.py
@@ -12,7 +12,7 @@
 SWEEPS = 2
 HALO = 8
 LANES = 128
-OFFSETS = (-2, -1, 1, 2)
+OFFSETS = (-1, 1, -2, 2)
 MESH = pl.DeviceIdType.MESH
 
 slope_resist = 4.0
@@ -54,6 +54,17 @@
     return jnp.dot(lhs, rhs, preferred_element_type=jnp.float32)
 
 
+def partner(me, step, count):
+    if count & (count - 1):
+        return lax.rem(me + step, count)
+    place, bit = 0, 1
+    while bit < count:
+        digit = lax.rem(me // bit, 2)
+        place = place + bit * (1 - digit if step & bit else digit)
+        bit *= 2
+    return place
+
+
 def iota(shape, dim):
     return lax.broadcasted_iota(jnp.int32, shape, dim)
 
@@ -68,8 +79,7 @@
     psi_hbm,
     row_freqs_hbm,
     col_freqs_hbm,
-    base_hbm,
-    flow_hbm,
+    out_hbm,
     phi_ref,
     target_ref,
     kernels_ref,
@@ -97,7 +107,7 @@
     grad,
     slope_ref,
     level_ref,
-    flow_ref,
+    out_ref,
     store_sem,
     mask_send,
     mask_recv,
@@ -246,10 +256,12 @@
             src, slot = phi_ref.at[:HALO], 1
         return to_strip(src, halo.at[slot], halo_send.at[slot], halo_recv.at[slot], offset)
 
+    even = lax.rem(strip, 2) == 0
+
     def send_spec(chunk):
-        for offset in (1, -1):
-
-            @pl.when(inside(offset))
+        for side, offset in ((even, 1), (even, -1), (jnp.logical_not(even), -1), (jnp.logical_not(even), 1)):
+
+            @pl.when(jnp.logical_and(side, inside(offset)))
             def _(offset=offset):
                 spec_copy(offset, chunk).start()
 
@@ -418,8 +430,8 @@
 
     mine = focus // stride
     owner = lax.rem(focus, stride) == 0
-    for step in list(range(1, chunks)) + [0]:
-        chunk = lax.rem(mine + step, chunks)
+    for step in range(chunks - 1, -1, -1):
+        chunk = partner(mine, step, chunks)
         adjoint(chunk)
         if step:
             to_owner(chunk).start()
@@ -468,13 +480,13 @@
         return to_strip(y_sum, y_side.at[slot], side_send.at[slot], side_recv.at[slot], offset)
 
     def gather_copy(step):
-        peer = lax.rem(focus + step, planes)
+        peer = partner(focus, step, planes)
         return to_focus(z_ref.at[mine], z_ref.at[mine], ag_send.at[step], ag_recv.at[mine], peer)
 
     def own_part():
         total = y_send[mine].astype(jnp.float32)
         for step in range(1, planes):
-            source = lax.rem(focus + step, planes)
+            source = partner(focus, step, planes)
             to_focus(
                 y_send.at[0], y_recv.at[source], rs_send.at[0], rs_recv.at[source], source
             ).wait_recv()
@@ -499,7 +511,7 @@
 
             rows_z += dot(row_out[index + 1], y_side[index])
         z_ref[mine] = jnp.concatenate([rows_z[:ext], -rows_z[ext:]], axis=1).astype(bf16)
-        for step in range(1, planes):
+        for step in range(planes - 1, 0, -1):
             gather_copy(step).start()
 
     if stride > 1:
@@ -513,7 +525,7 @@
         ).wait_recv()
 
     for step in range(chunks):
-        chunk = lax.rem(mine + step, chunks)
+        chunk = partner(mine, step, chunks)
         if step:
             arrived(chunk)
         elif stride > 1:
@@ -537,20 +549,14 @@
     empty = jnp.zeros((ext, LANES), jnp.float32)
     blocks = cols // LANES
     span = max(1, blocks // 4)
-    last = (SWEEPS - 1) % 2
 
     def store(part):
         here = slice(part * span * LANES, (part + 1) * span * LANES)
         return pltpu.make_async_copy(
-            flow_ref.at[:, here], flow_hbm.at[:, here], store_sem.at[1 + part]
-        )
-
-    store_base = pltpu.make_async_copy(
-        level_ref.at[last, HALO : HALO + rows], base_hbm, store_sem.at[0]
-    )
+            out_ref.at[:, here], out_hbm.at[:, here], store_sem.at[part]
+        )
+
     for sweep in range(SWEEPS):
-        if sweep == SWEEPS - 1:
-            store_base.start()
 
         def load(block, sweep=sweep):
             if not 0 <= block < blocks:
@@ -579,12 +585,11 @@
             if sweep < SWEEPS - 1:
                 level_ref[(sweep + 1) % 2, :, there] = (level + flow) * kept
             else:
-                flow_ref[:, there] = flow[HALO : HALO + rows]
+                out_ref[:, there] = (level + flow)[HALO : HALO + rows]
                 if (block + 1) % span == 0:
                     store(block // span).start()
             before, now, after = now, after, load(block + 2)
 
-    store_base.wait()
     for part in range(blocks // span):
         store(part).wait()
 
@@ -597,7 +602,7 @@
                 spec_copy(offset, chunk).wait_send()
 
     for step in range(chunks):
-        chunk = lax.rem(mine + step, chunks)
+        chunk = partner(mine, step, chunks)
         if step:
             to_owner(chunk).wait_send()
         elif stride > 1:
@@ -620,6 +625,23 @@
         pl.when(owner)(own_sent)
     else:
         own_sent()
+
+
+def deliver(src_ref, dst_ref, sem):
+    parts = sem.shape[0]
+    depth = src_ref.shape[0] // parts
+    copies = [
+        pltpu.make_async_copy(
+            src_ref.at[part * depth : (part + 1) * depth],
+            dst_ref.at[part * depth : (part + 1) * depth],
+            sem.at[part],
+        )
+        for part in range(parts)
+    ]
+    for copy in copies:
+        copy.start()
+    for copy in copies:
+        copy.wait()
 
 
 def on_device(strips, planes, phi, target, defocus_ids, kernels, psi, row_freqs, col_freqs):
@@ -632,11 +654,11 @@
     hbm = pl.BlockSpec(memory_space=pltpu.HBM)
     smem = pl.BlockSpec(memory_space=pltpu.SMEM)
     bf16, f32 = jnp.bfloat16, jnp.float32
-    base, flow = pl.pallas_call(
+    level = pl.pallas_call(
         functools.partial(kernel, strips, planes),
-        out_shape=[jax.ShapeDtypeStruct((rows, cols), f32)] * 2,
+        out_shape=jax.ShapeDtypeStruct((rows, cols), f32),
         in_specs=[smem] + [hbm] * 6,
-        out_specs=[hbm, hbm],
+        out_specs=hbm,
         scratch_shapes=[
             pltpu.VMEM(phi.shape, phi.dtype),
             pltpu.VMEM(target.shape, target.dtype),
@@ -666,7 +688,7 @@
             pltpu.VMEM((ext, cols), f32),
             pltpu.VMEM((2, ext, cols), f32),
             pltpu.VMEM((rows, cols), f32),
-            pltpu.SemaphoreType.DMA((1 + cols // LANES,)),
+            pltpu.SemaphoreType.DMA((cols // LANES,)),
             pltpu.SemaphoreType.DMA((2, chunks)),
             pltpu.SemaphoreType.DMA((2, chunks)),
             pltpu.SemaphoreType.DMA((2,)),
@@ -687,7 +709,14 @@
             transcendentals=0,
         ),
     )(defocus_ids, phi, target, kernels, psi, row_freqs[None], col_freqs[None])
-    return base + flow
+    return pl.pallas_call(
+        deliver,
+        out_shape=jax.ShapeDtypeStruct((rows, cols), f32),
+        in_specs=[hbm],
+        out_specs=hbm,
+        scratch_shapes=[pltpu.SemaphoreType.DMA((rows // HALO,))],
+        compiler_params=pltpu.CompilerParams(vmem_limit_bytes=58 * 2**20),
+    )(level)
 
 
 def solution(mesh):

time: 35.5 us -> 50.7 us (1.43)
  Pallas kernels: 32.7 us -> 49.9 us
  other arithmetic: 2.05 us -> 0 us
    pallas_call x1 -> x2, Pallas kernels: 32.7 us -> 49.9 us  [the longest x1 32.8 us: on_device(): pl.pallas_call(functools.partial(kernel, strips, planes), out_shape=jax.S...]
    add x1 -> x0, other arithmetic: 2.05 us -> none  [on_device(): return base + flow]
where the time goes in v4:
time: 50.7 us; the launch traced here: 50.6 us
  Pallas kernels  49.9 us (98%)
  between operations  0.66 us (1%)
    pallas_call x1, Pallas kernels, on_device(): pl.pallas_call(functools.partial(kernel, strips, planes), out_shape=jax.S...  32.8 us
    pallas_call x1, Pallas kernels, on_device(): pl.pallas_call(deliver, out_shape=jax.ShapeDtypeStruct((rows, cols), f32)...  17.1 us

profile of v4, /device:TPU:0, one launch (start us, length us, event | category | flops | bytes accessed | tf_op | source)
XLA Modules:
  0.0 50.6 jit_solution(10224113603166164192)
XLA Ops:
  0.7 32.8 %shard_map.73.src_ref = f32[64,2048]{1,0:T(8,128)} custom-call(s32[1]{0:T(128)S(6)} %copy.8.defocus_ref, f32[64,2048]{1,0:T(8,128)} %phi_hbm.1, s32[64,2048]{1,0:T(8,128)} %target_hbm.1, f32[2,4,48,512]{3,2,1,0:T(8,128)} %kernels_hbm.1, f32[48,512]{1,0:T(8,128)} %psi_hbm.1, s32[1,48]{1,0:T(1,128)} %bitcast.3, s32[1,512]{1,0:T(1,128)} %bitcast.2), custom_call_target="tpu_custom_call" | custom-call | flops 5435817984 | bytes 2359296 | tf_op jit(solution)/shard_map/pallas_call | solution.py:657
  33.5 17.1 %shard_map.74 = f32[64,2048]{1,0:T(8,128)} custom-call(f32[64,2048]{1,0:T(8,128)} %shard_map.73.src_ref), custom_call_target="tpu_custom_call" | custom-call | tf_op jit(solution)/shard_map/pallas_call | solution.py:712

commit v5 on v4

--- a/solution.py
+++ b/solution.py
@@ -192,24 +192,35 @@
 
     col_load.wait()
     col_lane = col_freqs_ref[...].astype(jnp.float32)
-    for block in range(fc // LANES):
-        freq_col[block * LANES : (block + 1) * LANES, :] = jnp.broadcast_to(
-            col_lane[:, block * LANES : (block + 1) * LANES], (LANES, LANES)
-        ).T
+    turn_lane = turn_pair(whole_turns(col_lane * float(LANES), float(cols)))
+    sign_lane = 1.0 - 2.0 * (col_lane - 2.0 * jnp.floor(0.5 * col_lane))
+    for index, values in enumerate((col_lane, turn_lane[0], turn_lane[1], sign_lane)):
+        for block in range(fc // LANES):
+            here = slice(block * LANES, (block + 1) * LANES)
+            freq_col[index, here, :] = jnp.broadcast_to(values[:, here], (LANES, LANES)).T
     group = 32
+    middle_col = cols // 2
 
     def table_rows(chunk):
         @pl.loop(0, wide // group)
         def _(step):
             first = pl.multiple_of(step * group, group)
-            freq = freq_col[pl.ds(chunk * wide + first, group), :]
+            spot = pl.ds(chunk * wide + first, group)
+            freq = freq_col[0, spot, :]
+            cos_turn, sin_turn = freq_col[1, spot, :], freq_col[2, spot, :]
+            sign = freq_col[3, spot, :].astype(bf16)
+            at_cos = pl.ds(2 * chunk * wide + first, group)
+            at_sin = pl.ds((2 * chunk + 1) * wide + first, group)
             lane = iota((group, LANES), 1).astype(jnp.float32)
             cos_now, sin_now = turn_pair(whole_turns(freq * lane, float(cols)))
-            cos_turn, sin_turn = turn_pair(whole_turns(freq * float(LANES), float(cols)))
-            for part in range(cols // LANES):
+            for part in range(middle_col // LANES):
                 here = slice(part * LANES, (part + 1) * LANES)
-                table[pl.ds(2 * chunk * wide + first, group), here] = cos_now.astype(bf16)
-                table[pl.ds((2 * chunk + 1) * wide + first, group), here] = sin_now.astype(bf16)
+                beyond = slice(middle_col + part * LANES, middle_col + (part + 1) * LANES)
+                cos_low, sin_low = cos_now.astype(bf16), sin_now.astype(bf16)
+                table[at_cos, here] = cos_low
+                table[at_sin, here] = sin_low
+                table[at_cos, beyond] = cos_low * sign
+                table[at_sin, beyond] = sin_low * sign
                 cos_now, sin_now = (
                     cos_now * cos_turn - sin_now * sin_turn,
                     sin_now * cos_turn + cos_now * sin_turn,
@@ -220,17 +231,26 @@
     def table_columns(block):
         freq = jnp.broadcast_to(col_lane[:, block * LANES : (block + 1) * LANES], (group, LANES))
         cos_turn, sin_turn = turn_pair(whole_turns(freq * float(group), float(cols)))
-        at_cos = 2 * (block * LANES // wide) * wide + block * LANES % wide
-
-        @pl.loop(0, cols // segment)
+        sign = jnp.broadcast_to(
+            sign_lane[:, block * LANES : (block + 1) * LANES], (group, LANES)
+        ).astype(bf16)
+        first_cos = 2 * (block * LANES // wide) * wide + block * LANES % wide
+        at_cos = slice(first_cos, first_cos + LANES)
+        at_sin = slice(first_cos + wide, first_cos + wide + LANES)
+
+        @pl.loop(0, middle_col // segment)
         def _(step):
             first = pl.multiple_of(step * segment, segment)
             place = (first + iota((group, LANES), 0)).astype(jnp.float32)
             cos_now, sin_now = turn_pair(whole_turns(freq * place, float(cols)))
             for part in range(segment // group):
                 here = pl.ds(first + part * group, group)
-                table_t[here, at_cos : at_cos + LANES] = cos_now.astype(bf16)
-                table_t[here, at_cos + wide : at_cos + wide + LANES] = sin_now.astype(bf16)
+                beyond = pl.ds(middle_col + first + part * group, group)
+                cos_low, sin_low = cos_now.astype(bf16), sin_now.astype(bf16)
+                table_t[here, at_cos] = cos_low
+                table_t[here, at_sin] = sin_low
+                table_t[beyond, at_cos] = cos_low * sign
+                table_t[beyond, at_sin] = sin_low * sign
                 cos_now, sin_now = (
                     cos_now * cos_turn - sin_now * sin_turn,
                     sin_now * cos_turn + cos_now * sin_turn,
@@ -627,21 +647,25 @@
         own_sent()
 
 
-def deliver(src_ref, dst_ref, sem):
-    parts = sem.shape[0]
+def deliver(src_ref, dst_ref, held, load_sem, store_sem):
+    parts = load_sem.shape[0]
     depth = src_ref.shape[0] // parts
-    copies = [
-        pltpu.make_async_copy(
-            src_ref.at[part * depth : (part + 1) * depth],
-            dst_ref.at[part * depth : (part + 1) * depth],
-            sem.at[part],
-        )
-        for part in range(parts)
+    spots = [slice(part * depth, (part + 1) * depth) for part in range(parts)]
+    loads = [
+        pltpu.make_async_copy(src_ref.at[spot], held.at[spot], load_sem.at[part])
+        for part, spot in enumerate(spots)
     ]
-    for copy in copies:
-        copy.start()
-    for copy in copies:
-        copy.wait()
+    stores = [
+        pltpu.make_async_copy(held.at[spot], dst_ref.at[spot], store_sem.at[part])
+        for part, spot in enumerate(spots)
+    ]
+    for load in loads:
+        load.start()
+    for load, store in zip(loads, stores):
+        load.wait()
+        store.start()
+    for store in stores:
+        store.wait()
 
 
 def on_device(strips, planes, phi, target, defocus_ids, kernels, psi, row_freqs, col_freqs):
@@ -669,7 +693,7 @@
             pltpu.SemaphoreType.DMA((6,)),
             pltpu.VMEM((2 * fc, cols), bf16),
             pltpu.VMEM((cols, 2 * fc), bf16),
-            pltpu.VMEM((fc, LANES), f32),
+            pltpu.VMEM((4, fc, LANES), f32),
             pltpu.VMEM((rows, cols), bf16),
             pltpu.VMEM((2, HALO, cols), f32),
             pltpu.VMEM((kern, chunks, fr, wide), f32),
@@ -714,7 +738,11 @@
         out_shape=jax.ShapeDtypeStruct((rows, cols), f32),
         in_specs=[hbm],
         out_specs=hbm,
-        scratch_shapes=[pltpu.SemaphoreType.DMA((rows // HALO,))],
+        scratch_shapes=[
+            pltpu.VMEM((rows, cols), f32),
+            pltpu.SemaphoreType.DMA((4,)),
+            pltpu.SemaphoreType.DMA((4,)),
+        ],
         compiler_params=pltpu.CompilerParams(vmem_limit_bytes=58 * 2**20),
     )(level)
 

time: 50.7 us -> 35.3 us (0.70)
  Pallas kernels: 49.9 us -> 34.3 us
    pallas_call x1, Pallas kernels: 17.1 us -> 1.82 us  [on_device(): pl.pallas_call(deliver, out_shape=jax.ShapeDtypeStruct((rows, cols), f32)...]
where the time goes in v5:
time: 35.3 us; the launch traced here: 35.1 us
  Pallas kernels  34.3 us (97%)
  between operations  0.82 us (2%)
    pallas_call x1, Pallas kernels, on_device(): pl.pallas_call(functools.partial(kernel, strips, planes), out_shape=jax.S...  32.5 us
    pallas_call x1, Pallas kernels, on_device(): pl.pallas_call(deliver, out_shape=jax.ShapeDtypeStruct((rows, cols), f32)...  1.82 us

profile of v5, /device:TPU:0, one launch (start us, length us, event | category | flops | bytes accessed | tf_op | source)
XLA Modules:
  0.0 35.1 jit_solution(8311860710564649172)
XLA Ops:
  0.7 32.5 %shard_map.73.src_ref = f32[64,2048]{1,0:T(8,128)} custom-call(s32[1]{0:T(128)S(6)} %copy.8.defocus_ref, f32[64,2048]{1,0:T(8,128)} %phi_hbm.1, s32[64,2048]{1,0:T(8,128)} %target_hbm.1, f32[2,4,48,512]{3,2,1,0:T(8,128)} %kernels_hbm.1, f32[48,512]{1,0:T(8,128)} %psi_hbm.1, s32[1,48]{1,0:T(1,128)} %bitcast.3, s32[1,512]{1,0:T(1,128)} %bitcast.2), custom_call_target="tpu_custom_call" | custom-call | flops 5435817984 | bytes 2359296 | tf_op jit(solution)/shard_map/pallas_call | solution.py:681
  33.1 1.8 %shard_map.74 = f32[64,2048]{1,0:T(8,128)} custom-call(f32[64,2048]{1,0:T(8,128)} %shard_map.73.src_ref), custom_call_target="tpu_custom_call" | custom-call | tf_op jit(solution)/shard_map/pallas_call | solution.py:736
